TPU v7x, 256 devices: a whole 4x4x8 slice. The times are simulated.
256 devices in a mesh: gz: 128 (over y, x_lo, z, core), gy: 2 (over x_hi).
Axes of the slice: x: 4 (x_hi: 2, x_lo: 2; x = x_hi * 2 + x_lo), y: 4, z: 8, core: 2. Of those that a mesh axis runs over, the one named last changes fastest.
Arguments:
- sensitivity: float32 [1024, 128, 512], P('gz', 'gy'), may hold values from -70 to 70
- density: float32 [1024, 128, 512], P('gz', 'gy'), may hold values from 0 to 1
- load: float32 [1024, 128, 512], P('gz', 'gy'), may hold values from -6 to 6
- adjoint: float32 [1024, 128, 512], P('gz', 'gy'), may hold values from -6 to 6
- labels: int32 [1024, 128, 512], P('gz', 'gy'), may hold values from 0 to 2
Outputs:
- update_direction: float32 [1024, 128, 512], P('gz', 'gy')
- adjoint_next: float32 [1024, 128, 512], P('gz', 'gy')
Inputs may be any that keep to these rules, and one draw needn't show every extreme that they name: `labels`: 0 marks a design voxel, 1 fixed masonry, 2 a supported voxel.
All inputs are finite; a program needn't handle non-finite values.
Results may differ from a plain program's by a relative error of at most 0.0003.
Values sent between devices are 32-bit elements; how exact they have to be, the bound alone decides.
A program may use at most 64 MiB of HBM per device.

v0:
```python
import jax
import jax.numpy as jnp
from jax import lax
from jax.sharding import PartitionSpec as P

ITERS = 4


filter_weight = 8.0
stiff_floor = 0.05
relax_omega = 0.6
volume_target = 0.15
volume_penalty = 20.0
epsilon = 1e-06
center_diag = 1.0 + 6.0 * filter_weight
lower_eig = 1.0 / center_diag
upper_eig = (1.0 + 12.0 * filter_weight) / center_diag
middle_eig = (upper_eig + lower_eig) / 2.0
half_width = (upper_eig - lower_eig) / 2.0
sigma_ratio = middle_eig / half_width


def with_halo(array, sides, width):
    for axis, dim in sides:
        size, length = (lax.axis_size(axis), array.shape[dim])
        up = [(i, (i + 1) % size) for i in range(size - 1)]
        down = [(j, i) for i, j in up]
        last = lax.slice_in_dim(array, length - width, length, axis=dim)
        leading = lax.slice_in_dim(array, 0, width, axis=dim)
        before = lax.ppermute(last, axis, up)
        after = lax.ppermute(leading, axis, down)
        array = jnp.concatenate([before, array, after], axis=dim)
    return array


def neighbour_sum(padded):
    total = padded[2:, 1:-1, 1:-1] + padded[:-2, 1:-1, 1:-1]
    total = total + padded[1:-1, 2:, 1:-1] + padded[1:-1, :-2, 1:-1]
    return total + padded[1:-1, 1:-1, 2:] + padded[1:-1, 1:-1, :-2]


def chebyshev(source, apply_fn, inside):
    residue = source
    update = inside * (source / (center_diag * middle_eig))
    result = update
    ratio_prev = 1.0 / sigma_ratio
    for iteration in range(ITERS):
        residue = residue - apply_fn(update)
        ratio_next = 1.0 / (2.0 * sigma_ratio - ratio_prev)
        update = inside * (
            ratio_next * ratio_prev * update
            + 2.0 * ratio_next / half_width * (residue / center_diag)
        )
        ratio_prev = ratio_next
        result = result + update
    return result


def stencil_sweep(padded_adj, padded_stiff, adjoint, stiffness, load, support):
    shape = adjoint.shape
    diagonal = jnp.zeros(shape, jnp.float32)
    offsum = jnp.zeros(shape, jnp.float32)
    for shift_z in (-1, 0, 1):
        for shift_y in (-1, 0, 1):
            for shift_x in (-1, 0, 1):
                nonzero = abs(shift_z) + abs(shift_y) + abs(shift_x)
                if nonzero == 0:
                    continue
                weight = {1: 1.0, 2: 0.5, 3: 0.25}[nonzero]
                near_adj = padded_adj[
                    1 + shift_z : 1 + shift_z + shape[0],
                    1 + shift_y : 1 + shift_y + shape[1],
                    1 + shift_x : 1 + shift_x + shape[2],
                ]
                near_stiff = padded_stiff[
                    1 + shift_z : 1 + shift_z + shape[0],
                    1 + shift_y : 1 + shift_y + shape[1],
                    1 + shift_x : 1 + shift_x + shape[2],
                ]
                coupling = weight * 0.5 * (stiffness + near_stiff)
                diagonal = diagonal + coupling
                offsum = offsum + coupling * near_adj
    applied = diagonal * adjoint - offsum
    updated = adjoint + relax_omega * (load - applied) / diagonal
    return jnp.where(support, 0.0, updated)


def on_device(sensitivity, density, load, adjoint, labels):
    design = labels == 0
    rows_z = sensitivity.shape[0]
    rows_y = sensitivity.shape[1]
    length = sensitivity.shape[2]
    volume_local = jnp.sum(jnp.where(design, density, 0.0))
    volume = lax.psum(volume_local, ("gz", "gy"))
    stiffness = stiff_floor + (1.0 - stiff_floor) * density**3

    def apply_each(field):
        padded = with_halo(field, (("gz", 0), ("gy", 1)), 1)
        padded = jnp.pad(padded, ((0, 0), (0, 0), (1, 1)))
        return center_diag * field - filter_weight * neighbour_sum(padded)

    smoothed = chebyshev(sensitivity, apply_each, 1.0)
    paired = jnp.stack((adjoint, stiffness))
    padded = with_halo(paired, (("gz", 1), ("gy", 2)), 1)
    padded = jnp.pad(padded, ((0, 0), (0, 0), (0, 0), (1, 1)))
    adjoint_padded = padded[0]
    stiff_padded = padded[1]
    filtered = jnp.where(design, smoothed, 0.0)
    magnitude_local = jnp.sum(jnp.abs(filtered))
    magnitude = lax.psum(magnitude_local, ("gz", "gy"))
    cells = float(rows_z * lax.axis_size("gz") * rows_y * lax.axis_size("gy") * length)
    update_direction = jnp.where(
        design,
        filtered / (magnitude / cells + epsilon)
        - volume_penalty * (volume / cells - volume_target),
        0.0,
    )
    adjoint_next = stencil_sweep(
        adjoint_padded, stiff_padded, adjoint, stiffness, load, labels == 2
    )
    return (update_direction, adjoint_next)


def solution(mesh):
    placed = (
        P("gz", "gy", None),
        P("gz", "gy", None),
        P("gz", "gy", None),
        P("gz", "gy", None),
        P("gz", "gy", None),
    )
    return jax.shard_map(
        on_device,
        mesh=mesh,
        in_specs=placed,
        out_specs=(P("gz", "gy", None), P("gz", "gy", None)),
        check_vma=False,
    )
```

profile of v0, /device:TPU:1, one launch (start us, length us, event | category | flops | bytes accessed | tf_op | source)
XLA Modules:
  0.0 210.6 jit_solution(10339587554247225588)
XLA Ops:
  0.6 1.3 broadcast_multiply_fusion
  2.0 4.9 %collective-permute-start.1 = (f32[1,64,512]{2,1,0:T(8,128)S(1)}, f32[1,64,512]{2,1,0:T(8,128)S(1)}, u32[]{:S(2)}, u32[]{:S(2)}) collective-permute-start(f32[1,64,512]{2,1,0:T(8,128)S(1)} %get-tuple-element.33), channel_id=1, source_target_pairs={{0,2},{2,4},{4,6},{6,8},{8,10},{10,12},{12,14},{14,16},{16,18},{18... | collective-permute-start | bytes 393224 | tf_op jit(solution)/shard_map/ppermute | solution.py:30
  6.9 1.9 collective-permute-start
  8.9 0.0 collective-permute-done.1
  8.9 4.3 %collective-permute-done = f32[1,64,512]{2,1,0:T(8,128)S(1)} collective-permute-done((f32[1,64,512]{2,1,0:T(8,128)S(1)}, f32[1,64,512]{2,1,0:T(8,128)S(1)}, u32[]{:S(2)}, u32[]{:S(2)}) %collective-permute-start) | collective-permute-done | bytes 131104 | tf_op jit(solution)/shard_map/ppermute | solution.py:31
  13.3 0.0 copy-start.1
  13.3 4.8 %collective-permute-start.3 = (f32[10,1,512]{2,1,0:T(1,128)S(1)}, f32[10,1,512]{2,1,0:T(1,128)S(1)}, u32[]{:S(2)}, u32[]{:S(2)}) collective-permute-start(f32[10,1,512]{2,1,0:T(1,128)S(1)} %get-tuple-element.23), channel_id=1, source_target_pairs={{0,1},{2,3},{4,5},{6,7},{8,9},{10,11},{12,13},{14,15},{16,17},{18,... | collective-permute-start | bytes 61448 | tf_op jit(solution)/shard_map/ppermute | solution.py:30
  18.1 1.3 collective-permute-start.2
  19.4 0.0 collective-permute-done.3
  19.4 4.7 %collective-permute-done.2 = f32[10,1,512]{2,1,0:T(1,128)S(1)} collective-permute-done((f32[10,1,512]{2,1,0:T(1,128)S(1)}, f32[10,1,512]{2,1,0:T(1,128)S(1)}, u32[]{:S(2)}, u32[]{:S(2)}) %collective-permute-start.2) | collective-permute-done | bytes 20512 | tf_op jit(solution)/shard_map/ppermute | solution.py:31
  24.1 0.7 select_maximum_fusion.17
  24.8 0.9 multiply_add_fusion.2
  25.7 3.2 %collective-permute-start.5 = (f32[1,64,512]{2,1,0:T(8,128)S(1)}, f32[1,64,512]{2,1,0:T(8,128)S(1)}, u32[]{:S(2)}, u32[]{:S(2)}) collective-permute-start(f32[1,64,512]{2,1,0:T(8,128)S(1)} %get-tuple-element.31), channel_id=1, source_target_pairs={{0,2},{2,4},{4,6},{6,8},{8,10},{10,12},{12,14},{14,16},{16,18},{18... | collective-permute-start | bytes 393224 | tf_op jit(solution)/shard_map/ppermute | solution.py:30
  29.0 1.9 collective-permute-start.4
  30.9 0.0 collective-permute-done.5
  30.9 4.3 %collective-permute-done.4 = f32[1,64,512]{2,1,0:T(8,128)S(1)} collective-permute-done((f32[1,64,512]{2,1,0:T(8,128)S(1)}, f32[1,64,512]{2,1,0:T(8,128)S(1)}, u32[]{:S(2)}, u32[]{:S(2)}) %collective-permute-start.4) | collective-permute-done | bytes 131104 | tf_op jit(solution)/shard_map/ppermute | solution.py:31
  35.3 1.4 collective-permute-start.7
  36.6 1.3 collective-permute-start.6
  37.9 0.0 collective-permute-done.7
  38.0 4.7 %collective-permute-done.6 = f32[10,1,512]{2,1,0:T(1,128)S(1)} collective-permute-done((f32[10,1,512]{2,1,0:T(1,128)S(1)}, f32[10,1,512]{2,1,0:T(1,128)S(1)}, u32[]{:S(2)}, u32[]{:S(2)}) %collective-permute-start.6) | collective-permute-done | bytes 20512 | tf_op jit(solution)/shard_map/ppermute | solution.py:31
  42.7 0.7 select_maximum_fusion.13
  43.4 0.9 multiply_add_fusion.1
  44.3 3.2 %collective-permute-start.9 = (f32[1,64,512]{2,1,0:T(8,128)S(1)}, f32[1,64,512]{2,1,0:T(8,128)S(1)}, u32[]{:S(2)}, u32[]{:S(2)}) collective-permute-start(f32[1,64,512]{2,1,0:T(8,128)S(1)} %get-tuple-element.29), channel_id=1, source_target_pairs={{0,2},{2,4},{4,6},{6,8},{8,10},{10,12},{12,14},{14,16},{16,18},{18... | collective-permute-start | bytes 393224 | tf_op jit(solution)/shard_map/ppermute | solution.py:30
  47.5 1.9 collective-permute-start.8
  49.5 0.0 collective-permute-done.9
  49.5 4.3 %collective-permute-done.8 = f32[1,64,512]{2,1,0:T(8,128)S(1)} collective-permute-done((f32[1,64,512]{2,1,0:T(8,128)S(1)}, f32[1,64,512]{2,1,0:T(8,128)S(1)}, u32[]{:S(2)}, u32[]{:S(2)}) %collective-permute-start.8) | collective-permute-done | bytes 131104 | tf_op jit(solution)/shard_map/ppermute | solution.py:31
  53.9 1.4 collective-permute-start.11
  55.2 1.3 collective-permute-start.10
  56.5 0.0 collective-permute-done.11
  56.5 4.7 %collective-permute-done.10 = f32[10,1,512]{2,1,0:T(1,128)S(1)} collective-permute-done((f32[10,1,512]{2,1,0:T(1,128)S(1)}, f32[10,1,512]{2,1,0:T(1,128)S(1)}, u32[]{:S(2)}, u32[]{:S(2)}) %collective-permute-start.10) | collective-permute-done | bytes 20512 | tf_op jit(solution)/shard_map/ppermute | solution.py:31
  61.3 0.7 select_maximum_fusion.9
  62.0 0.9 multiply_add_fusion
  62.9 3.2 %collective-permute-start.13 = (f32[1,64,512]{2,1,0:T(8,128)S(1)}, f32[1,64,512]{2,1,0:T(8,128)S(1)}, u32[]{:S(2)}, u32[]{:S(2)}) collective-permute-start(f32[1,64,512]{2,1,0:T(8,128)S(1)} %get-tuple-element.27), channel_id=1, source_target_pairs={{0,2},{2,4},{4,6},{6,8},{8,10},{10,12},{12,14},{14,16},{16,18},{18... | collective-permute-start | bytes 393224 | tf_op jit(solution)/shard_map/ppermute | solution.py:30
  66.1 1.9 collective-permute-start.12
  68.0 0.0 collective-permute-done.13
  68.0 4.3 %collective-permute-done.12 = f32[1,64,512]{2,1,0:T(8,128)S(1)} collective-permute-done((f32[1,64,512]{2,1,0:T(8,128)S(1)}, f32[1,64,512]{2,1,0:T(8,128)S(1)}, u32[]{:S(2)}, u32[]{:S(2)}) %collective-permute-start.12) | collective-permute-done | bytes 131104 | tf_op jit(solution)/shard_map/ppermute | solution.py:31
  72.4 0.0 copy-start.2
  72.4 1.8 collective-permute-start.15
  74.2 1.3 collective-permute-start.14
  75.5 0.0 collective-permute-done.15
  75.5 4.7 %collective-permute-done.14 = f32[10,1,512]{2,1,0:T(1,128)S(1)} collective-permute-done((f32[10,1,512]{2,1,0:T(1,128)S(1)}, f32[10,1,512]{2,1,0:T(1,128)S(1)}, u32[]{:S(2)}, u32[]{:S(2)}) %collective-permute-start.14) | collective-permute-done | bytes 20512 | tf_op jit(solution)/shard_map/ppermute | solution.py:31
  80.3 0.7 select_maximum_fusion.5
  81.0 0.0 copy-start.3
  81.0 4.4 %abs_reduce_fusion = (f32[]{:T(128)}, f32[8,64,512]{2,1,0:T(8,128)}, pred[8,64,512]{2,1,0:T(8,128)(4,1)S(1)}) fusion(f32[10,66,514]{2,1,0:T(8,128)S(1)} %select_maximum_fusion.5, f32[1,64,512]{2,1,0:T(8,128)S(1)} %collective-permute-done.12, f32[8,64,512]{2,1,0:T(8,128)S(1)} %multiply_add_fusion, f32[1,64,512]{2,1,0:T(8,128)S(1)} %collective-permute-done.13, ...), kind=kLoop, calls=%fused_computation.210 | loop fusion | flops 12058623 | bytes 12402692 | tf_op jit(solution)/shard_map/reduce_sum | solution.py:109
  85.5 0.9 fusion.87
  86.4 0.3 copy-done
  86.7 0.8 pad_maximum_fusion.33
  87.5 3.2 %collective-permute-start.16 = (f32[2,1,64,512]{3,2,1,0:T(8,128)}, f32[2,1,64,512]{3,2,1,0:T(8,128)}, u32[]{:S(2)}, u32[]{:S(2)}) collective-permute-start(f32[2,1,64,512]{3,2,1,0:T(8,128)} %get-tuple-element.15), channel_id=1, source_target_pairs={{0,2},{2,4},{4,6},{6,8},{8,10},{10,12},{12,14},{14,16},{16,18},{18... | collective-permute-start | bytes 786440 | tf_op jit(solution)/shard_map/ppermute | solution.py:30
  90.7 1.9 collective-permute-start.17
  92.6 89.6 %all-reduce.5 = (f32[]{:T(128)}, f32[]{:T(128)}) all-reduce(f32[]{:T(128)} %get-tuple-element.26, f32[]{:T(128)} %get-tuple-element.4), channel_id=1, replica_groups=mesh['gz'=128,'gy'=2] {'gz','gy'}, use_global_device_ids=true, to_apply=%region_3.4 | all-reduce | flops 2 | bytes 16 | tf_op jit(solution)/shard_map/psum | solution.py:94
  183.4 0.0 copy-start.5
  183.4 0.0 collective-permute-done.16
  183.4 1.0 pad_maximum_fusion.37
  184.4 3.1 %collective-permute-start.18 = (f32[2,10,1,512]{3,2,1,0:T(1,128)S(1)}, f32[2,10,1,512]{3,2,1,0:T(1,128)S(1)}, u32[]{:S(2)}, u32[]{:S(2)}) collective-permute-start(f32[2,10,1,512]{3,2,1,0:T(1,128)S(1)} %get-tuple-element.13), channel_id=1, source_target_pairs={{0,1},{2,3},{4,5},{6,7},{8,9},{10,11},{12,13},{14,15},{16,17},{18,... | collective-permute-start | bytes 122888 | tf_op jit(solution)/shard_map/ppermute | solution.py:30
  187.5 1.5 collective-permute-start.19
  188.9 1.2 subtract_select_fusion
  190.1 3.6 %collective-permute-done.19 = f32[2,10,1,512]{3,2,1,0:T(1,128)S(1)} collective-permute-done((f32[2,10,1,512]{3,2,1,0:T(1,128)S(1)}, f32[2,10,1,512]{3,2,1,0:T(1,128)S(1)}, u32[]{:S(2)}, u32[]{:S(2)}) %collective-permute-start.19) | collective-permute-done | bytes 40992 | tf_op jit(solution)/shard_map/ppermute | solution.py:31
  193.7 4.7 %select_maximum_fusion = f32[2,10,66,514]{3,2,1,0:T(8,128)S(1)} fusion(f32[2,10,1,512]{3,2,1,0:T(1,128)S(1)} %collective-permute-done.19, f32[2,10,1,512]{3,2,1,0:T(1,128)S(1)} %collective-permute-done.18, f32[2,1,64,512]{3,2,1,0:T(8,128)} %collective-permute-done.17, f32[2,1,64,512]{3,2,1,0:T(8,128)} %collective-permute-done.16, ...), kind=kLoop, calls=%fused_computation.2 | loop fusion | flops 9498720 | bytes 5417280 | tf_op jit(solution)/shard_map/concatenate | solution.py:32
  198.4 0.0 copy-start.4
  198.5 0.0 copy-start.6
  198.5 0.2 slice_bitcast_fusion.1
  198.7 1.0 copy-done.4
  199.7 0.3 copy-done.6
  200.0 10.6 %fusion.10 = f32[8,64,512]{2,1,0:T(8,128)} fusion(f32[8,64,512]{2,1,0:T(8,128)S(1)} %copy-done, f32[8,64,512]{2,1,0:T(8,128)S(1)} %copy-done.6, f32[10,66,514]{2,1,0:T(8,128)S(1)} %get-tuple-element.12, f32[10,66,514]{2,1,0:T(8,128)S(1)} %get-tuple-element.11, s32[8,64,512]{2,1,0:T(8,128)S(1)} %copy-done.2, f32[8,64,512]{2,1,0:T(8,128)S(1)} %copy-done.4), kind=kLoop, calls=%fused_computation.40 | loop fusion | flops 36700160 | bytes 59768832 | tf_op jit(solution)/shard_map/jit(_where)/select_n | solution.py:85
  (15 shorter events, 0.2 us)
Async XLA Ops:
  2.0 6.9 %collective-permute-start.1 = (f32[1,64,512]{2,1,0:T(8,128)S(1)}, f32[1,64,512]{2,1,0:T(8,128)S(1)}, u32[]{:S(2)}, u32[]{:S(2)}) collective-permute-start(f32[1,64,512]{2,1,0:T(8,128)S(1)} %get-tuple-element.33), channel_id=1, source_target_pairs={{0,2},{2,4},{4,6},{6,8},{8,10},{10,12},{12,14},{14,16},{16,18},{18... | collective-permute-start | bytes 393224 | tf_op jit(solution)/shard_map/ppermute | solution.py:30
  6.9 6.3 %collective-permute-start = (f32[1,64,512]{2,1,0:T(8,128)S(1)}, f32[1,64,512]{2,1,0:T(8,128)S(1)}, u32[]{:S(2)}, u32[]{:S(2)}) collective-permute-start(f32[1,64,512]{2,1,0:T(8,128)S(1)} %get-tuple-element.34), channel_id=1, source_target_pairs={{2,0},{4,2},{6,4},{8,6},{10,8},{12,10},{14,12},{16,14},{18,16},{20... | collective-permute-start | bytes 393224 | tf_op jit(solution)/shard_map/ppermute | solution.py:31
  13.3 11.6 %copy-start.1 = (f32[8,64,512]{2,1,0:T(8,128)S(1)}, f32[8,64,512]{2,1,0:T(8,128)}, u32[]{:S(2)}) copy-start(f32[8,64,512]{2,1,0:T(8,128)} %param.5) | copy-start | bytes 3145732
  13.3 6.1 %collective-permute-start.3 = (f32[10,1,512]{2,1,0:T(1,128)S(1)}, f32[10,1,512]{2,1,0:T(1,128)S(1)}, u32[]{:S(2)}, u32[]{:S(2)}) collective-permute-start(f32[10,1,512]{2,1,0:T(1,128)S(1)} %get-tuple-element.23), channel_id=1, source_target_pairs={{0,1},{2,3},{4,5},{6,7},{8,9},{10,11},{12,13},{14,15},{16,17},{18,... | collective-permute-start | bytes 61448 | tf_op jit(solution)/shard_map/ppermute | solution.py:30
  18.1 6.0 %collective-permute-start.2 = (f32[10,1,512]{2,1,0:T(1,128)S(1)}, f32[10,1,512]{2,1,0:T(1,128)S(1)}, u32[]{:S(2)}, u32[]{:S(2)}) collective-permute-start(f32[10,1,512]{2,1,0:T(1,128)S(1)} %get-tuple-element.24), channel_id=1, source_target_pairs={{1,0},{3,2},{5,4},{7,6},{9,8},{11,10},{13,12},{15,14},{17,16},{19,... | collective-permute-start | bytes 61448 | tf_op jit(solution)/shard_map/ppermute | solution.py:31
  25.7 5.2 %collective-permute-start.5 = (f32[1,64,512]{2,1,0:T(8,128)S(1)}, f32[1,64,512]{2,1,0:T(8,128)S(1)}, u32[]{:S(2)}, u32[]{:S(2)}) collective-permute-start(f32[1,64,512]{2,1,0:T(8,128)S(1)} %get-tuple-element.31), channel_id=1, source_target_pairs={{0,2},{2,4},{4,6},{6,8},{8,10},{10,12},{12,14},{14,16},{16,18},{18... | collective-permute-start | bytes 393224 | tf_op jit(solution)/shard_map/ppermute | solution.py:30
  29.0 6.3 %collective-permute-start.4 = (f32[1,64,512]{2,1,0:T(8,128)S(1)}, f32[1,64,512]{2,1,0:T(8,128)S(1)}, u32[]{:S(2)}, u32[]{:S(2)}) collective-permute-start(f32[1,64,512]{2,1,0:T(8,128)S(1)} %get-tuple-element.32), channel_id=1, source_target_pairs={{2,0},{4,2},{6,4},{8,6},{10,8},{12,10},{14,12},{16,14},{18,16},{20... | collective-permute-start | bytes 393224 | tf_op jit(solution)/shard_map/ppermute | solution.py:31
  35.3 2.7 %collective-permute-start.7 = (f32[10,1,512]{2,1,0:T(1,128)S(1)}, f32[10,1,512]{2,1,0:T(1,128)S(1)}, u32[]{:S(2)}, u32[]{:S(2)}) collective-permute-start(f32[10,1,512]{2,1,0:T(1,128)S(1)} %get-tuple-element.21), channel_id=1, source_target_pairs={{0,1},{2,3},{4,5},{6,7},{8,9},{10,11},{12,13},{14,15},{16,17},{18,... | collective-permute-start | bytes 61448 | tf_op jit(solution)/shard_map/ppermute | solution.py:30
  36.6 6.0 %collective-permute-start.6 = (f32[10,1,512]{2,1,0:T(1,128)S(1)}, f32[10,1,512]{2,1,0:T(1,128)S(1)}, u32[]{:S(2)}, u32[]{:S(2)}) collective-permute-start(f32[10,1,512]{2,1,0:T(1,128)S(1)} %get-tuple-element.22), channel_id=1, source_target_pairs={{1,0},{3,2},{5,4},{7,6},{9,8},{11,10},{13,12},{15,14},{17,16},{19,... | collective-permute-start | bytes 61448 | tf_op jit(solution)/shard_map/ppermute | solution.py:31
  44.3 5.2 %collective-permute-start.9 = (f32[1,64,512]{2,1,0:T(8,128)S(1)}, f32[1,64,512]{2,1,0:T(8,128)S(1)}, u32[]{:S(2)}, u32[]{:S(2)}) collective-permute-start(f32[1,64,512]{2,1,0:T(8,128)S(1)} %get-tuple-element.29), channel_id=1, source_target_pairs={{0,2},{2,4},{4,6},{6,8},{8,10},{10,12},{12,14},{14,16},{16,18},{18... | collective-permute-start | bytes 393224 | tf_op jit(solution)/shard_map/ppermute | solution.py:30
  47.5 6.3 %collective-permute-start.8 = (f32[1,64,512]{2,1,0:T(8,128)S(1)}, f32[1,64,512]{2,1,0:T(8,128)S(1)}, u32[]{:S(2)}, u32[]{:S(2)}) collective-permute-start(f32[1,64,512]{2,1,0:T(8,128)S(1)} %get-tuple-element.30), channel_id=1, source_target_pairs={{2,0},{4,2},{6,4},{8,6},{10,8},{12,10},{14,12},{16,14},{18,16},{20... | collective-permute-start | bytes 393224 | tf_op jit(solution)/shard_map/ppermute | solution.py:31
  53.9 2.7 %collective-permute-start.11 = (f32[10,1,512]{2,1,0:T(1,128)S(1)}, f32[10,1,512]{2,1,0:T(1,128)S(1)}, u32[]{:S(2)}, u32[]{:S(2)}) collective-permute-start(f32[10,1,512]{2,1,0:T(1,128)S(1)} %get-tuple-element.19), channel_id=1, source_target_pairs={{0,1},{2,3},{4,5},{6,7},{8,9},{10,11},{12,13},{14,15},{16,17},{18,... | collective-permute-start | bytes 61448 | tf_op jit(solution)/shard_map/ppermute | solution.py:30
  55.2 6.0 %collective-permute-start.10 = (f32[10,1,512]{2,1,0:T(1,128)S(1)}, f32[10,1,512]{2,1,0:T(1,128)S(1)}, u32[]{:S(2)}, u32[]{:S(2)}) collective-permute-start(f32[10,1,512]{2,1,0:T(1,128)S(1)} %get-tuple-element.20), channel_id=1, source_target_pairs={{1,0},{3,2},{5,4},{7,6},{9,8},{11,10},{13,12},{15,14},{17,16},{19,... | collective-permute-start | bytes 61448 | tf_op jit(solution)/shard_map/ppermute | solution.py:31
  62.9 5.2 %collective-permute-start.13 = (f32[1,64,512]{2,1,0:T(8,128)S(1)}, f32[1,64,512]{2,1,0:T(8,128)S(1)}, u32[]{:S(2)}, u32[]{:S(2)}) collective-permute-start(f32[1,64,512]{2,1,0:T(8,128)S(1)} %get-tuple-element.27), channel_id=1, source_target_pairs={{0,2},{2,4},{4,6},{6,8},{8,10},{10,12},{12,14},{14,16},{16,18},{18... | collective-permute-start | bytes 393224 | tf_op jit(solution)/shard_map/ppermute | solution.py:30
  66.1 6.3 %collective-permute-start.12 = (f32[1,64,512]{2,1,0:T(8,128)S(1)}, f32[1,64,512]{2,1,0:T(8,128)S(1)}, u32[]{:S(2)}, u32[]{:S(2)}) collective-permute-start(f32[1,64,512]{2,1,0:T(8,128)S(1)} %get-tuple-element.28), channel_id=1, source_target_pairs={{2,0},{4,2},{6,4},{8,6},{10,8},{12,10},{14,12},{16,14},{18,16},{20... | collective-permute-start | bytes 393224 | tf_op jit(solution)/shard_map/ppermute | solution.py:31
  72.4 8.6 %copy-start.2 = (s32[8,64,512]{2,1,0:T(8,128)S(1)}, s32[8,64,512]{2,1,0:T(8,128)}, u32[]{:S(2)}) copy-start(s32[8,64,512]{2,1,0:T(8,128)} %param.9) | copy-start | bytes 3145732
  72.4 3.1 %collective-permute-start.15 = (f32[10,1,512]{2,1,0:T(1,128)S(1)}, f32[10,1,512]{2,1,0:T(1,128)S(1)}, u32[]{:S(2)}, u32[]{:S(2)}) collective-permute-start(f32[10,1,512]{2,1,0:T(1,128)S(1)} %get-tuple-element.17), channel_id=1, source_target_pairs={{0,1},{2,3},{4,5},{6,7},{8,9},{10,11},{12,13},{14,15},{16,17},{18,... | collective-permute-start | bytes 61448 | tf_op jit(solution)/shard_map/ppermute | solution.py:30
  74.2 6.0 %collective-permute-start.14 = (f32[10,1,512]{2,1,0:T(1,128)S(1)}, f32[10,1,512]{2,1,0:T(1,128)S(1)}, u32[]{:S(2)}, u32[]{:S(2)}) collective-permute-start(f32[10,1,512]{2,1,0:T(1,128)S(1)} %get-tuple-element.18), channel_id=1, source_target_pairs={{1,0},{3,2},{5,4},{7,6},{9,8},{11,10},{13,12},{15,14},{17,16},{19,... | collective-permute-start | bytes 61448 | tf_op jit(solution)/shard_map/ppermute | solution.py:31
  81.0 4.5 %copy-start.3 = (f32[8,64,512]{2,1,0:T(8,128)S(1)}, f32[8,64,512]{2,1,0:T(8,128)}, u32[]{:S(2)}) copy-start(f32[8,64,512]{2,1,0:T(8,128)} %param.6) | copy-start | bytes 3145732
  85.5 1.2 copy-start
  87.5 95.9 %collective-permute-start.16 = (f32[2,1,64,512]{3,2,1,0:T(8,128)}, f32[2,1,64,512]{3,2,1,0:T(8,128)}, u32[]{:S(2)}, u32[]{:S(2)}) collective-permute-start(f32[2,1,64,512]{3,2,1,0:T(8,128)} %get-tuple-element.15), channel_id=1, source_target_pairs={{0,2},{2,4},{4,6},{6,8},{8,10},{10,12},{12,14},{14,16},{16,18},{18... | collective-permute-start | bytes 786440 | tf_op jit(solution)/shard_map/ppermute | solution.py:30
  90.7 92.7 %collective-permute-start.17 = (f32[2,1,64,512]{3,2,1,0:T(8,128)}, f32[2,1,64,512]{3,2,1,0:T(8,128)}, u32[]{:S(2)}, u32[]{:S(2)}) collective-permute-start(f32[2,1,64,512]{3,2,1,0:T(8,128)} %get-tuple-element.16), channel_id=1, source_target_pairs={{2,0},{4,2},{6,4},{8,6},{10,8},{12,10},{14,12},{16,14},{18,16},{20... | collective-permute-start | bytes 786440 | tf_op jit(solution)/shard_map/ppermute | solution.py:31
  183.4 5.6 %copy-start.5 = (f32[8,64,512]{2,1,0:T(8,128)S(1)}, f32[8,64,512]{2,1,0:T(8,128)}, u32[]{:S(2)}) copy-start(f32[8,64,512]{2,1,0:T(8,128)} %get-tuple-element.5) | copy-start | bytes 3145732
  184.4 5.8 %collective-permute-start.18 = (f32[2,10,1,512]{3,2,1,0:T(1,128)S(1)}, f32[2,10,1,512]{3,2,1,0:T(1,128)S(1)}, u32[]{:S(2)}, u32[]{:S(2)}) collective-permute-start(f32[2,10,1,512]{3,2,1,0:T(1,128)S(1)} %get-tuple-element.13), channel_id=1, source_target_pairs={{0,1},{2,3},{4,5},{6,7},{8,9},{10,11},{12,13},{14,15},{16,17},{18,... | collective-permute-start | bytes 122888 | tf_op jit(solution)/shard_map/ppermute | solution.py:30
  187.5 6.3 %collective-permute-start.19 = (f32[2,10,1,512]{3,2,1,0:T(1,128)S(1)}, f32[2,10,1,512]{3,2,1,0:T(1,128)S(1)}, u32[]{:S(2)}, u32[]{:S(2)}) collective-permute-start(f32[2,10,1,512]{3,2,1,0:T(1,128)S(1)} %get-tuple-element.14), channel_id=1, source_target_pairs={{1,0},{3,2},{5,4},{7,6},{9,8},{11,10},{13,12},{15,14},{17,16},{19,... | collective-permute-start | bytes 122888 | tf_op jit(solution)/shard_map/ppermute | solution.py:31
  198.4 1.2 copy-start.4
  198.5 1.5 copy-start.6
where the time goes:
time: 212 us; the launch traced here: 211 us
  blocking collectives  89.6 us (42%)
  starting transfers between devices  46.4 us (22%)
  waiting for transfers between devices  39.9 us (19%)
  other arithmetic  30.6 us (14%)
  between operations  2.24 us (1%)
    psum x1, blocking collectives, on_device(): volume = lax.psum(volume_local, ('gz', 'gy'))  89.6 us
    ppermute x10, waiting for transfers between devices, with_halo(): after = lax.ppermute(leading, axis, down)  39.9 us
    ppermute x10, starting transfers between devices, with_halo(): before = lax.ppermute(last, axis, up)  30.1 us
    ppermute x10, starting transfers between devices, with_halo(): after = lax.ppermute(leading, axis, down)  16.2 us
    select_n x1, other arithmetic, stencil_sweep(): return jnp.where(support, 0.0, updated)  10.6 us
    concatenate x9, other arithmetic, with_halo(): array = jnp.concatenate([before, array, after], axis=dim)  7.76 us
    reduce_sum x1, other arithmetic, on_device(): magnitude_local = jnp.sum(jnp.abs(filtered))  4.44 us
  transfers between devices with their start and end apart: 20, of which 9 were waited for; matrix products, arithmetic and copies ran while one was open for 1% of the time, Pallas kernels for 0%

commit v1 on v0

v1 whole, which is shorter than its diff:
```python
import functools

import numpy as np
import jax
import jax.numpy as jnp
from jax import lax
from jax.experimental import pallas as pl
from jax.experimental.pallas import tpu as pltpu
from jax.sharding import PartitionSpec as P

ITERS = 4
filter_weight = 8.0
stiff_floor = 0.05
relax_omega = 0.6
volume_target = 0.15
volume_penalty = 20.0
epsilon = 1e-06
center_diag = 1.0 + 6.0 * filter_weight
lower_eig = 1.0 / center_diag
upper_eig = (1.0 + 12.0 * filter_weight) / center_diag
middle_eig = (upper_eig + lower_eig) / 2.0
half_width = (upper_eig - lower_eig) / 2.0
sigma_ratio = middle_eig / half_width

MESH = pl.DeviceIdType.MESH
F32 = jnp.float32

CZ, CY, NX = 8, 64, 512
GZ, GY = 128, 2
GROUP = 16
ROWS = CY + 24
DEEP = ITERS
FZ = CZ + 2 * DEEP


def filter_coefficients():
    times_t = np.polynomial.chebyshev.chebmulx
    residue = np.zeros(ITERS + 2)
    residue[0] = 1.0

    def pad(series):
        return np.pad(series, (0, max(0, ITERS + 2 - len(series))))[: ITERS + 2]

    def apply(series):
        return center_diag * (middle_eig * series + half_width * pad(times_t(series)))

    update = residue / (center_diag * middle_eig)
    result = update.copy()
    ratio_prev = 1.0 / sigma_ratio
    for _ in range(ITERS):
        residue = residue - apply(update)
        ratio_next = 1.0 / (2.0 * sigma_ratio - ratio_prev)
        update = ratio_next * ratio_prev * update + 2.0 * ratio_next / half_width * (
            residue / center_diag
        )
        ratio_prev = ratio_next
        result = result + update
    return [float(value) for value in result[: ITERS + 1]]


GAMMA = filter_coefficients()
SELF = (1.0 - middle_eig) / half_width
NEAR = filter_weight / (center_diag * half_width)


def lane_edge(width, at):
    return lax.broadcasted_iota(jnp.int32, (width, 128), 1) == at


def shift_lanes(value):
    rows = value.shape[0]
    left = pltpu.roll(value, 1, 1)
    right = pltpu.roll(value, NX - 1, 1)
    first = jnp.where(lane_edge(rows, 0), 0.0, left[:, :128])
    last = jnp.where(lane_edge(rows, 127), 0.0, right[:, NX - 128 :])
    left = jnp.concatenate([first, left[:, 128:]], axis=1)
    right = jnp.concatenate([right[:, : NX - 128], last], axis=1)
    return left, right


def load_rows(ref, plane, start, rows):
    wide = ref[plane, pl.ds(start - 8, rows + 16), :]
    above = pltpu.roll(wide, 1, 0)[8 : 8 + rows]
    below = pltpu.roll(wide, rows + 15, 0)[8 : 8 + rows]
    return wide[8 : 8 + rows], above, below


def near_sum(ref, plane, start, rows):
    middle, above, below = load_rows(ref, plane, start, rows)
    left, right = shift_lanes(middle)
    over = ref[plane - 1, pl.ds(start, rows), :] + ref[plane + 1, pl.ds(start, rows), :]
    return middle, over + (above + below) + (left + right)


def main_kernel(
    sens, dens, load, adj, labels,
    filt_out, adj_out, lab_out, tot_out,
    e, b3, b2, b1, ud, stiff, prod, line, load_v, mine, got,
    in_sem, lo_send, lo_recv, hi_send, hi_recv, side_send, side_recv, ud_send, ud_recv, ar_send, ar_recv,
):
    z = lax.axis_index("gz")
    y = lax.axis_index("gy")
    up = (lax.rem(z + 1, GZ), y)
    down = (lax.rem(z + GZ - 1, GZ), y)
    side = (z, 1 - y)
    side_up = (up[0], 1 - y)
    side_down = (down[0], 1 - y)
    block = z // GROUP
    rank = lax.rem(z, GROUP)
    plane_rank = block * GY + y
    groups = ([], [])
    for d in range(1, GROUP):
        groups[0].append((block * GROUP + lax.rem(rank + d, GROUP), y))
        other = lax.rem(plane_rank + d, GROUP)
        groups[1].append(((other // GY) * GROUP + rank, lax.rem(other, GY)))

    partner = pl.ds(pl.multiple_of(72 - 64 * y, 8), 8)
    e[:, partner, :] = jnp.zeros((FZ, 8, NX), F32)
    ud[:, :, partner, :] = jnp.zeros((2, CZ + 2, 8, NX), F32)

    barrier = pltpu.get_barrier_semaphore()
    greeted = [up, down, side, side_up, side_down] + groups[0] + groups[1]
    for device in greeted:
        pl.semaphore_signal(barrier, inc=1, device_id=device, device_id_type=MESH)

    own = pl.multiple_of(8 + 8 * y, 8)
    mine_rows = pl.ds(own, CY)
    loads = [
        pltpu.make_async_copy(sens, e.at[pl.ds(DEEP, CZ), mine_rows, :], in_sem.at[0]),
        pltpu.make_async_copy(labels, lab_out, in_sem.at[1]),
        pltpu.make_async_copy(dens, ud.at[1, pl.ds(1, CZ), mine_rows, :], in_sem.at[2]),
        pltpu.make_async_copy(adj, ud.at[0, pl.ds(1, CZ), mine_rows, :], in_sem.at[3]),
        pltpu.make_async_copy(load, load_v, in_sem.at[4]),
    ]
    for copy in loads:
        copy.start()

    def clear(plane, _):
        zero = jnp.zeros((8, NX), F32)
        for ref in (e, b3, b2, b1):
            ref[plane, 0:8, :] = zero
            ref[plane, 80:88, :] = zero
        return 0

    lax.fori_loop(0, FZ, clear, 0)

    def clear_two(plane, _):
        zero = jnp.zeros((8, NX), F32)
        for ref in (ud.at[0], stiff, prod):
            ref[plane, 0:8, :] = zero
            ref[plane, 80:88, :] = zero
        return 0

    lax.fori_loop(0, CZ + 2, clear_two, 0)

    four_from = 68 - 52 * y
    four_to = 12 + 60 * y
    four_src = pl.ds(four_from, DEEP)
    four_dst = pl.ds(four_to, DEEP)

    def remote(src, dst, send, recv, device):
        return pltpu.make_async_remote_copy(src, dst, send, recv, device_id=device, device_id_type=MESH)

    side_copies = [
        remote(e.at[pl.ds(4, 8), four_src, :], e.at[pl.ds(4, 8), four_dst, :], side_send.at[0], side_recv.at[0], side),
        remote(e.at[pl.ds(8, 4), four_src, :], e.at[pl.ds(0, 4), four_dst, :], side_send.at[1], side_recv.at[1], side_up),
        remote(e.at[pl.ds(4, 4), four_src, :], e.at[pl.ds(12, 4), four_dst, :], side_send.at[2], side_recv.at[2], side_down),
    ]
    up_copies, down_copies = [], []
    for d in range(1, DEEP + 1):
        to_up, to_down = DEEP - d, DEEP + CZ - 1 + d
        up_copies.append(
            remote(e.at[to_up + CZ, mine_rows, :], e.at[to_up, mine_rows, :], lo_send.at[d - 1], lo_recv.at[d - 1], up)
        )
        down_copies.append(
            remote(e.at[to_down - CZ, mine_rows, :], e.at[to_down, mine_rows, :], hi_send.at[d - 1], hi_recv.at[d - 1], down)
        )

    one_from = 71 - 55 * y
    one_to = 15 + 57 * y
    one_src = pl.ds(one_from, 1)
    one_dst = pl.ds(one_to, 1)
    both = pl.ds(0, 2)
    ud_copies = [
        remote(ud.at[both, CZ, mine_rows, :], ud.at[both, 0, mine_rows, :], ud_send.at[0], ud_recv.at[0], up),
        remote(ud.at[both, 1, mine_rows, :], ud.at[both, CZ + 1, mine_rows, :], ud_send.at[1], ud_recv.at[1], down),
        remote(ud.at[both, pl.ds(1, CZ), one_src, :], ud.at[both, pl.ds(1, CZ), one_dst, :], ud_send.at[2], ud_recv.at[2], side),
        remote(ud.at[both, CZ, one_src, :], ud.at[both, 0, one_dst, :], ud_send.at[3], ud_recv.at[3], side_up),
        remote(ud.at[both, 1, one_src, :], ud.at[both, CZ + 1, one_dst, :], ud_send.at[4], ud_recv.at[4], side_down),
    ]

    loads[0].wait()
    pl.semaphore_wait(barrier, len(greeted))
    for d in range(DEEP):
        up_copies[d].start()
        down_copies[d].start()
        if d == 0:
            for copy in side_copies:
                copy.start()

    loads[1].wait()
    loads[2].wait()

    def volume_plane(plane, total):
        value = jnp.where(lab_out[plane] == 0, ud[1, plane + 1, mine_rows, :], 0.0)
        return total + jnp.sum(value.reshape(CY // 8, 8, NX), axis=0)

    volume = lax.fori_loop(0, CZ, volume_plane, jnp.zeros((8, NX), F32))
    loads[3].wait()
    loads[4].wait()

    def level3(plane, keep):
        for start in (8, 32, 56):
            middle, near = near_sum(e, plane, start, 24)
            value = (GAMMA[3] + 2.0 * SELF * GAMMA[4]) * middle - (2.0 * NEAR * GAMMA[4]) * near
            b3[plane, pl.ds(start, 24), :] = value * keep

    def level2(plane, keep):
        for start in (8, 32, 56):
            middle, near = near_sum(b3, plane, start, 24)
            value = (GAMMA[2] - GAMMA[4]) * e[plane, pl.ds(start, 24), :] - (2.0 * NEAR) * near
            if SELF != 0.0:
                value = value + (2.0 * SELF) * middle
            b2[plane, pl.ds(start, 24), :] = value * keep

    def level1(plane, keep):
        for start in (8, 32, 56):
            middle, near = near_sum(b2, plane, start, 24)
            value = GAMMA[1] * e[plane, pl.ds(start, 24), :] - b3[plane, pl.ds(start, 24), :] - (2.0 * NEAR) * near
            if SELF != 0.0:
                value = value + (2.0 * SELF) * middle
            b1[plane, pl.ds(start, 24), :] = value * keep

    def level0(plane, total):
        for part in range(CY // 16):
            start = pl.multiple_of(own + 16 * part, 8)
            rows = pl.ds(start, 16)
            middle, near = near_sum(b1, plane, start, 16)
            value = GAMMA[0] * e[plane, rows, :] - b2[plane, rows, :] - NEAR * near
            if SELF != 0.0:
                value = value + SELF * middle
            value = jnp.where(lab_out[plane - DEEP, 16 * part : 16 * part + 16, :] == 0, value, 0.0)
            filt_out[plane - DEEP, 16 * part : 16 * part + 16, :] = value
            size = jnp.abs(value)
            total = total + (size[:8] + size[8:])
        return total

    def keep_of(plane):
        outside = ((plane < DEEP) & (z == 0)) | ((plane >= DEEP + CZ) & (z == GZ - 1))
        return jnp.where(outside, 0.0, 1.0).astype(F32)

    def repeat(level, first, last):
        def body(plane, _):
            level(plane, 1.0)
            return 0

        lax.fori_loop(first, last, body, 0)

    side_copies[0].wait_recv()
    repeat(level3, 5, 11)
    repeat(level2, 6, 10)
    repeat(level1, 7, 9)
    side_copies[1].wait_recv()
    side_copies[2].wait_recv()

    total = jnp.zeros((8, NX), F32)
    for d in range(1, DEEP + 1):
        up_copies[d - 1].wait_recv()
        down_copies[d - 1].wait_recv()
        if d == 3:
            for copy in ud_copies:
                copy.start()

        @pl.when(z == 0)
        def _():
            e[DEEP - d] = jnp.zeros((ROWS, NX), F32)

        @pl.when(z == GZ - 1)
        def _():
            e[DEEP + CZ - 1 + d] = jnp.zeros((ROWS, NX), F32)

        def wave(at, total):
            def plane_of(low):
                return low + at * (FZ - 1 - 2 * low)

            level3(plane_of(5 - d), keep_of(plane_of(5 - d)))
            level2(plane_of(6 - d), keep_of(plane_of(6 - d)))
            level1(plane_of(7 - d), keep_of(plane_of(7 - d)))
            return level0(plane_of(8 - d), total)

        total = lax.fori_loop(0, 2, wave, total)

    def fold(value):
        lanes = value[:, :128] + value[:, 128:256] + value[:, 256:384] + value[:, 384:]
        return jnp.sum(lanes, axis=0, keepdims=True)

    row = lax.broadcasted_iota(jnp.int32, (8, 128), 0)
    mine[0] = jnp.where(row < 4, fold(total), fold(volume))

    def spread(phase):
        for d in range(GROUP - 1):
            remote(mine.at[phase], got.at[phase, d], ar_send.at[phase], ar_recv.at[phase], groups[phase][d]).start()

    def gather(phase):
        pltpu.make_async_copy(got.at[phase], got.at[phase], ar_recv.at[phase]).wait()
        return mine[phase] + jnp.sum(got[phase], axis=0)

    spread(0)

    for copy in ud_copies:
        copy.wait_recv()

    def sweep_lines(plane, _):
        outside = ((plane == 0) & (z == 0)) | ((plane == CZ + 1) & (z == GZ - 1))
        keep = jnp.where(outside, 0.0, 1.0).astype(F32)
        for start in (8, 32, 56):
            rows = pl.ds(start, 24)
            density = ud[1, plane, rows, :]
            field = ud[0, plane, rows, :] * keep
            value = (stiff_floor + (1.0 - stiff_floor) * (density * density * density)) * keep
            stiff[plane, rows, :] = value
            prod[plane, rows, :] = value * field
            ud[0, plane, rows, :] = field
        for part in range(CY // 16):
            start = pl.multiple_of(own + 16 * part, 8)
            for slot, ref in enumerate((stiff, ud.at[0], prod)):
                middle, above, below = load_rows(ref, plane, start, 16)
                value = middle + 0.5 * (above + below)
                left, right = shift_lanes(value)
                line[slot, plane, 16 * part : 16 * part + 16, :] = value + 0.5 * (left + right)
        return 0

    for copy in ud_copies:
        copy.wait_send()
    lax.fori_loop(0, CZ + 2, sweep_lines, 0)

    mine[1] = gather(0)
    spread(1)

    def sweep_out(plane, _):
        for part in range(CY // 16):
            here = slice(16 * part, 16 * part + 16)
            rows = pl.ds(pl.multiple_of(own + 16 * part, 8), 16)

            def stack(slot):
                return line[slot, plane + 1, here, :] + 0.5 * (
                    line[slot, plane, here, :] + line[slot, plane + 2, here, :]
                )

            value = stiff[plane + 1, rows, :]
            field = ud[0, plane + 1, rows, :]
            diagonal = 6.0 * value + stack(0)
            offsum = value * stack(1) + (stack(2) - 2.0 * prod[plane + 1, rows, :])
            applied = diagonal * field - offsum
            updated = field + relax_omega * (load_v[plane, here, :] - applied) / diagonal
            adj_out[plane, here, :] = jnp.where(lab_out[plane, here, :] == 2, 0.0, updated)
        return 0

    lax.fori_loop(0, CZ, sweep_out, 0)

    tot_out[...] = gather(1)
    for phase in range(2):
        pltpu.make_async_copy(got.at[phase], got.at[phase], ar_send.at[phase]).wait()
    for copy in side_copies + up_copies + down_copies:
        copy.wait_send()


def last_kernel(filt, adj_in, labels, tot, dir_out, adj_out, held, sem):
    whole = pltpu.make_async_copy(adj_in, adj_out, sem.at[CZ])
    whole.start()
    cells = float(GZ * CZ * GY * CY * NX)
    magnitude = jnp.sum(tot[0:1, :], axis=1, keepdims=True)
    volume = jnp.sum(tot[4:5, :], axis=1, keepdims=True)
    scale = 1.0 / (magnitude / cells + epsilon)
    offset = volume_penalty * (volume / cells - volume_target)
    scale = jnp.broadcast_to(scale, (CY, NX))
    offset = jnp.broadcast_to(offset, (CY, NX))
    copies = []
    for plane in range(CZ):
        held[plane] = jnp.where(labels[plane] == 0, filt[plane] * scale - offset, 0.0)
        copy = pltpu.make_async_copy(held.at[plane], dir_out.at[plane], sem.at[plane])
        copy.start()
        copies.append(copy)
    for copy in copies + [whole]:
        copy.wait()


def on_device(sensitivity, density, load, adjoint, labels):
    shape = (CZ, CY, NX)
    dma = pltpu.SemaphoreType.DMA
    vmem = pl.BlockSpec(memory_space=pltpu.VMEM)
    hbm = pl.BlockSpec(memory_space=pltpu.HBM)
    filtered, swept, held_labels, totals = pl.pallas_call(
        main_kernel,
        out_shape=(
            jax.ShapeDtypeStruct(shape, F32),
            jax.ShapeDtypeStruct(shape, F32),
            jax.ShapeDtypeStruct(shape, jnp.int32),
            jax.ShapeDtypeStruct((8, 128), F32),
        ),
        in_specs=[hbm] * 5,
        out_specs=(vmem,) * 4,
        scratch_shapes=[
            pltpu.VMEM((FZ, ROWS, NX), F32),
            pltpu.VMEM((FZ, ROWS, NX), F32),
            pltpu.VMEM((FZ, ROWS, NX), F32),
            pltpu.VMEM((FZ, ROWS, NX), F32),
            pltpu.VMEM((2, CZ + 2, ROWS, NX), F32),
            pltpu.VMEM((CZ + 2, ROWS, NX), F32),
            pltpu.VMEM((CZ + 2, ROWS, NX), F32),
            pltpu.VMEM((3, CZ + 2, CY, NX), F32),
            pltpu.VMEM(shape, F32),
            pltpu.VMEM((2, 8, 128), F32),
            pltpu.VMEM((2, GROUP - 1, 8, 128), F32),
            dma((5,)),
            dma((DEEP,)),
            dma((DEEP,)),
            dma((DEEP,)),
            dma((DEEP,)),
            dma((3,)),
            dma((3,)),
            dma((5,)),
            dma((5,)),
            dma((2,)),
            dma((2,)),
        ],
        compiler_params=pltpu.CompilerParams(
            collective_id=1, has_side_effects=True, vmem_limit_bytes=40 * 2**20
        ),
        name="filter_and_sweep",
    )(sensitivity, density, load, adjoint, labels)
    return pl.pallas_call(
        last_kernel,
        out_shape=(jax.ShapeDtypeStruct(shape, F32), jax.ShapeDtypeStruct(shape, F32)),
        in_specs=[vmem] * 4,
        out_specs=(hbm, hbm),
        scratch_shapes=[pltpu.VMEM(shape, F32), dma((CZ + 1,))],
        name="normalise_and_store",
    )(filtered, swept, held_labels, totals)


def solution(mesh):
    placed = (P("gz", "gy", None),) * 5
    return jax.shard_map(
        on_device,
        mesh=mesh,
        in_specs=placed,
        out_specs=(P("gz", "gy", None), P("gz", "gy", None)),
        check_vma=False,
    )
```

time: 212 us -> 51.7 us (0.24)
  blocking collectives: 89.6 us -> 0 us
  starting transfers between devices: 46.4 us -> 0 us
  Pallas kernels: 0 us -> 40.5 us
  waiting for transfers between devices: 39.9 us -> 0 us
  other arithmetic: 30.6 us -> 0 us
  local copies, waits for them, and re-layouts: 1.95 us -> 9.66 us
    psum x1 -> x0, blocking collectives: 89.6 us -> none  [on_device(): volume = lax.psum(volume_local, ('gz', 'gy'))]
    ppermute x20 -> x0, starting transfers between devices: 46.4 us -> none  [the longest x10 30.1 us: with_halo(): before = lax.ppermute(last, axis, up)]
    pallas_call x0 -> x2, Pallas kernels: none -> 40.5 us  [the longest x1 37.2 us: on_device(): pl.pallas_call(main_kernel, out_shape=(jax.ShapeDtypeStruct(shape, F32),...]
    ppermute x20 -> x0, waiting for transfers between devices: 39.9 us -> none  [the longest x10 39.9 us: with_halo(): after = lax.ppermute(leading, axis, down)]
    select_n x2 -> x0, other arithmetic: 11.7 us -> none  [the longest x1 10.6 us: stencil_sweep(): return jnp.where(support, 0.0, updated)]
    unnamed x14 -> x18, local copies, waits for them, and re-layouts: 1.63 us -> 9.66 us
    concatenate x9 -> x0, other arithmetic: 7.76 us -> none  [with_halo(): array = jnp.concatenate([before, array, after], axis=dim)]
    reduce_sum x1 -> x0, other arithmetic: 4.44 us -> none  [on_device(): magnitude_local = jnp.sum(jnp.abs(filtered))]
  transfers between devices with their start and end apart: 20 -> 0, of which waited for: 9 -> 0; matrix products, arithmetic and copies ran while one was open for 1% -> 0% of each run, Pallas kernels for 0% -> 0%
where the time goes in v1:
time: 51.7 us; the launch traced here: 50.8 us
  Pallas kernels  40.5 us (78%)
  local copies, waits for them, and re-layouts  9.66 us (19%)
  between operations  0.66 us (1%)
    pallas_call x1, Pallas kernels, on_device(): pl.pallas_call(main_kernel, out_shape=(jax.ShapeDtypeStruct(shape, F32),...  37.2 us
    unnamed x18, local copies, waits for them, and re-layouts  9.66 us
    pallas_call x1, Pallas kernels, on_device(): pl.pallas_call(last_kernel, out_shape=(jax.ShapeDtypeStruct(shape, F32),...  3.24 us

profile of v1, /device:TPU:1, one launch (start us, length us, event | category | flops | bytes accessed | tf_op | source)
XLA Modules:
  0.0 50.8 jit_solution(8492110540334537323)
XLA Ops:
  0.6 0.0 copy-start
  0.6 1.2 %copy-done = f32[8,64,512]{2,1,0:T(8,128)S(1)} copy-done((f32[8,64,512]{2,1,0:T(8,128)S(1)}, f32[8,64,512]{2,1,0:T(8,128)}, u32[]{:S(2)}) %copy-start) | copy-done | bytes 1048600
  1.9 0.0 copy-start.1
  1.9 1.2 %copy-done.1 = f32[8,64,512]{2,1,0:T(8,128)S(1)} copy-done((f32[8,64,512]{2,1,0:T(8,128)S(1)}, f32[8,64,512]{2,1,0:T(8,128)}, u32[]{:S(2)}) %copy-start.1) | copy-done | bytes 1048600
  3.1 0.0 copy-start.2
  3.1 1.2 %copy-done.2 = f32[8,64,512]{2,1,0:T(8,128)S(1)} copy-done((f32[8,64,512]{2,1,0:T(8,128)S(1)}, f32[8,64,512]{2,1,0:T(8,128)}, u32[]{:S(2)}) %copy-start.2) | copy-done | bytes 1048600
  4.3 0.0 copy-start.3
  4.3 1.2 %copy-done.3 = f32[8,64,512]{2,1,0:T(8,128)S(1)} copy-done((f32[8,64,512]{2,1,0:T(8,128)S(1)}, f32[8,64,512]{2,1,0:T(8,128)}, u32[]{:S(2)}) %copy-start.3) | copy-done | bytes 1048600
  5.5 0.0 copy-start.4
  5.5 1.2 %copy-done.4 = s32[8,64,512]{2,1,0:T(8,128)S(1)} copy-done((s32[8,64,512]{2,1,0:T(8,128)S(1)}, s32[8,64,512]{2,1,0:T(8,128)}, u32[]{:S(2)}) %copy-start.4) | copy-done | bytes 1048600
  6.8 37.2 %filter_and_sweep.1 = (f32[8,64,512]{2,1,0:T(8,128)S(1)}, f32[8,64,512]{2,1,0:T(8,128)S(1)}, s32[8,64,512]{2,1,0:T(8,128)S(1)}, f32[8,128]{1,0:T(8,128)S(1)}) custom-call(f32[8,64,512]{2,1,0:T(8,128)S(1)} %copy-done, f32[8,64,512]{2,1,0:T(8,128)S(1)} %copy-done.1, f32[8,64,512]{2,1,0:T(8,128)S(1)} %copy-done.2, f32[8,64,512]{2,1,0:T(8,128)S(1)} %copy-done.3, ...), custom_call_target="tpu_custom_call" | custom-call | tf_op jit(solution)/shard_map/filter_and_sweep/pallas_call | solution.py:393
  44.0 0.0 copy-start.5
  44.0 1.0 %copy-done.5 = f32[8,64,512]{2,1,0:T(8,128)} copy-done((f32[8,64,512]{2,1,0:T(8,128)}, f32[8,64,512]{2,1,0:T(8,128)S(1)}, u32[]{:S(2)}) %copy-start.5) | copy-done | bytes 1048600
  45.0 0.0 copy-start.6
  45.0 1.0 %copy-done.6 = f32[8,64,512]{2,1,0:T(8,128)} copy-done((f32[8,64,512]{2,1,0:T(8,128)}, f32[8,64,512]{2,1,0:T(8,128)S(1)}, u32[]{:S(2)}) %copy-start.6) | copy-done | bytes 1048600
  46.0 0.0 copy-start.7
  46.0 1.0 %copy-done.7 = s32[8,64,512]{2,1,0:T(8,128)} copy-done((s32[8,64,512]{2,1,0:T(8,128)}, s32[8,64,512]{2,1,0:T(8,128)S(1)}, u32[]{:S(2)}) %copy-start.7) | copy-done | bytes 1048600
  47.0 0.0 copy-start.8
  47.0 0.6 %copy-done.8 = f32[8,128]{1,0:T(8,128)} copy-done((f32[8,128]{1,0:T(8,128)}, f32[8,128]{1,0:T(8,128)S(1)}, u32[]{:S(2)}) %copy-start.8) | copy-done | bytes 4120
  47.5 3.2 %normalise_and_store.1 = (f32[8,64,512]{2,1,0:T(8,128)}, f32[8,64,512]{2,1,0:T(8,128)}) custom-call(f32[8,64,512]{2,1,0:T(8,128)} %copy-done.5, f32[8,64,512]{2,1,0:T(8,128)} %copy-done.6, s32[8,64,512]{2,1,0:T(8,128)} %copy-done.7, f32[8,128]{1,0:T(8,128)} %copy-done.8), custom_call_target="tpu_custom_call" | custom-call | tf_op jit(solution)/shard_map/normalise_and_store/pallas_call | solution.py:432
Async XLA Ops:
  0.6 1.2 %copy-start = (f32[8,64,512]{2,1,0:T(8,128)S(1)}, f32[8,64,512]{2,1,0:T(8,128)}, u32[]{:S(2)}) copy-start(f32[8,64,512]{2,1,0:T(8,128)} %sens.1) | copy-start | bytes 3145732
  1.9 1.2 %copy-start.1 = (f32[8,64,512]{2,1,0:T(8,128)S(1)}, f32[8,64,512]{2,1,0:T(8,128)}, u32[]{:S(2)}) copy-start(f32[8,64,512]{2,1,0:T(8,128)} %dens.1) | copy-start | bytes 3145732
  3.1 1.2 %copy-start.2 = (f32[8,64,512]{2,1,0:T(8,128)S(1)}, f32[8,64,512]{2,1,0:T(8,128)}, u32[]{:S(2)}) copy-start(f32[8,64,512]{2,1,0:T(8,128)} %load.1) | copy-start | bytes 3145732
  4.3 1.2 %copy-start.3 = (f32[8,64,512]{2,1,0:T(8,128)S(1)}, f32[8,64,512]{2,1,0:T(8,128)}, u32[]{:S(2)}) copy-start(f32[8,64,512]{2,1,0:T(8,128)} %adj.1) | copy-start | bytes 3145732
  5.5 1.2 %copy-start.4 = (s32[8,64,512]{2,1,0:T(8,128)S(1)}, s32[8,64,512]{2,1,0:T(8,128)}, u32[]{:S(2)}) copy-start(s32[8,64,512]{2,1,0:T(8,128)} %labels.1) | copy-start | bytes 3145732
  44.0 1.0 %copy-start.5 = (f32[8,64,512]{2,1,0:T(8,128)}, f32[8,64,512]{2,1,0:T(8,128)S(1)}, u32[]{:S(2)}) copy-start(f32[8,64,512]{2,1,0:T(8,128)S(1)} %get-tuple-element.6.filt) | copy-start | bytes 3145732
  45.0 1.0 %copy-start.6 = (f32[8,64,512]{2,1,0:T(8,128)}, f32[8,64,512]{2,1,0:T(8,128)S(1)}, u32[]{:S(2)}) copy-start(f32[8,64,512]{2,1,0:T(8,128)S(1)} %get-tuple-element.7.adj_in) | copy-start | bytes 3145732
  46.0 1.0 %copy-start.7 = (s32[8,64,512]{2,1,0:T(8,128)}, s32[8,64,512]{2,1,0:T(8,128)S(1)}, u32[]{:S(2)}) copy-start(s32[8,64,512]{2,1,0:T(8,128)S(1)} %get-tuple-element.8.labels) | copy-start | bytes 3145732
  47.0 0.6 %copy-start.8 = (f32[8,128]{1,0:T(8,128)}, f32[8,128]{1,0:T(8,128)S(1)}, u32[]{:S(2)}) copy-start(f32[8,128]{1,0:T(8,128)S(1)} %get-tuple-element.9.tot) | copy-start | bytes 12292

commit v2 on v1

v2 whole, which is shorter than its diff:
```python
import functools

import numpy as np
import jax
import jax.numpy as jnp
from jax import lax
from jax.experimental import pallas as pl
from jax.experimental.pallas import tpu as pltpu
from jax.sharding import PartitionSpec as P

ITERS = 4
filter_weight = 8.0
stiff_floor = 0.05
relax_omega = 0.6
volume_target = 0.15
volume_penalty = 20.0
epsilon = 1e-06
center_diag = 1.0 + 6.0 * filter_weight
lower_eig = 1.0 / center_diag
upper_eig = (1.0 + 12.0 * filter_weight) / center_diag
middle_eig = (upper_eig + lower_eig) / 2.0
half_width = (upper_eig - lower_eig) / 2.0
sigma_ratio = middle_eig / half_width

MESH = pl.DeviceIdType.MESH
F32 = jnp.float32

CZ, CY, NX = 8, 64, 512
GZ, GY = 128, 2
GROUP = 16
ROWS = CY + 24
DEEP = ITERS
FZ = CZ + 2 * DEEP


def filter_coefficients():
    times_t = np.polynomial.chebyshev.chebmulx
    residue = np.zeros(ITERS + 2)
    residue[0] = 1.0

    def pad(series):
        return np.pad(series, (0, max(0, ITERS + 2 - len(series))))[: ITERS + 2]

    def apply(series):
        return center_diag * (middle_eig * series + half_width * pad(times_t(series)))

    update = residue / (center_diag * middle_eig)
    result = update.copy()
    ratio_prev = 1.0 / sigma_ratio
    for _ in range(ITERS):
        residue = residue - apply(update)
        ratio_next = 1.0 / (2.0 * sigma_ratio - ratio_prev)
        update = ratio_next * ratio_prev * update + 2.0 * ratio_next / half_width * (
            residue / center_diag
        )
        ratio_prev = ratio_next
        result = result + update
    return [float(value) for value in result[: ITERS + 1]]


GAMMA = filter_coefficients()
SELF = (1.0 - middle_eig) / half_width
NEAR = filter_weight / (center_diag * half_width)
TILES = NX // 128


def sine_basis():
    index = np.arange(1, NX + 1, dtype=np.float64)
    basis = np.sqrt(2.0 / (NX + 1)) * np.sin(np.pi * np.outer(index, index) / (NX + 1))
    high = basis.astype(jnp.bfloat16)
    low = (basis - high.astype(np.float64)).astype(jnp.bfloat16)
    along = 2.0 * np.cos(np.pi * index / (NX + 1))
    factors = np.zeros((8, NX))
    factors[0] = GAMMA[3] + 2.0 * GAMMA[4] * (SELF - NEAR * along)
    factors[1] = 2.0 * (SELF - NEAR * along)
    factors[2] = SELF - NEAR * along
    return np.stack([high, low]), factors.astype(np.float32)


BASIS, FACTORS = sine_basis()


def transform(value, basis):
    high = value.astype(jnp.bfloat16)
    low = (value - high.astype(F32)).astype(jnp.bfloat16)
    first = jnp.dot(high, basis[0], preferred_element_type=F32)
    second = jnp.dot(low, basis[0], preferred_element_type=F32)
    third = jnp.dot(high, basis[1], preferred_element_type=F32)
    return first + (second + third)


def smooth_lanes(tiles):
    lane = lax.broadcasted_iota(jnp.int32, tiles[0].shape, 1)
    from_left = [pltpu.roll(tile, 1, 1) for tile in tiles]
    from_right = [pltpu.roll(tile, 127, 1) for tile in tiles]
    out = []
    for j, tile in enumerate(tiles):
        left = jnp.where(lane == 0, from_left[j - 1] if j > 0 else 0.0, from_left[j])
        right = jnp.where(lane == 127, from_right[j + 1] if j + 1 < TILES else 0.0, from_right[j])
        out.append(tile + 0.5 * (left + right))
    return out


def main_kernel(
    sens, dens, load, adj, labels, basis_in, factors_in,
    filt_out, adj_out, lab_out, tot_out,
    raw, basis, factors, e, b3, b2, b1, flat, ud, stiff, smooth, column, load_v, mine, got,
    in_sem, lo_send, lo_recv, hi_send, hi_recv, side_send, side_recv, ud_send, ud_recv, ar_send, ar_recv,
):
    z = lax.axis_index("gz")
    y = lax.axis_index("gy")
    up = (lax.rem(z + 1, GZ), y)
    down = (lax.rem(z + GZ - 1, GZ), y)
    side = (z, 1 - y)
    side_up = (up[0], 1 - y)
    side_down = (down[0], 1 - y)
    block = z // GROUP
    rank = lax.rem(z, GROUP)
    plane_rank = block * GY + y
    groups = ([], [])
    for d in range(1, GROUP):
        groups[0].append((block * GROUP + lax.rem(rank + d, GROUP), y))
        other = lax.rem(plane_rank + d, GROUP)
        groups[1].append(((other // GY) * GROUP + rank, lax.rem(other, GY)))

    own = pl.multiple_of(8 + 8 * y, 8)
    mine_rows = pl.ds(own, CY)
    partner = pl.ds(pl.multiple_of(72 - 64 * y, 8), 8)
    all_tiles = pl.ds(0, TILES)
    loads = [
        pltpu.make_async_copy(sens, raw, in_sem.at[0]),
        pltpu.make_async_copy(basis_in, basis, in_sem.at[1]),
        pltpu.make_async_copy(factors_in, factors, in_sem.at[2]),
        pltpu.make_async_copy(labels, lab_out, in_sem.at[3]),
        pltpu.make_async_copy(load, load_v, in_sem.at[4]),
    ]
    for j in range(TILES):
        for slot, array in enumerate((adj, dens)):
            loads.append(
                pltpu.make_async_copy(
                    array.at[:, :, pl.ds(128 * j, 128)],
                    ud.at[slot, j, pl.ds(1, CZ), mine_rows, :],
                    in_sem.at[5 + 2 * j + slot],
                )
            )
    for copy in loads:
        copy.start()

    e[:, :, partner, :] = jnp.zeros((TILES, FZ, 8, 128), F32)
    ud[:, :, :, partner, :] = jnp.zeros((2, TILES, CZ + 2, 8, 128), F32)

    barrier = pltpu.get_barrier_semaphore()
    greeted = [up, down, side, side_up, side_down] + groups[0] + groups[1]
    for device in greeted:
        pl.semaphore_signal(barrier, inc=1, device_id=device, device_id_type=MESH)

    def clear(j, _):
        for ref in (e, b3, b2, b1):
            ref[j, :, 0:8, :] = jnp.zeros((FZ, 8, 128), F32)
            ref[j, :, 80:88, :] = jnp.zeros((FZ, 8, 128), F32)
        for slot in range(3):
            smooth[slot, j, :, 0:8, :] = jnp.zeros((CZ + 2, 8, 128), F32)
            smooth[slot, j, :, 80:88, :] = jnp.zeros((CZ + 2, 8, 128), F32)
            column[slot, j, 0:8, :] = jnp.zeros((8, 128), F32)
            column[slot, j, 80:88, :] = jnp.zeros((8, 128), F32)
        return 0

    lax.fori_loop(0, TILES, clear, 0)

    loads[0].wait()
    loads[1].wait()
    loads[2].wait()
    spectrum = transform(raw[...].reshape(CZ * CY, NX), basis)
    for plane in range(CZ):
        for j in range(TILES):
            e[j, DEEP + plane, mine_rows, :] = spectrum[CY * plane : CY * plane + CY, 128 * j : 128 * j + 128]

    four_src, four_dst = pl.ds(68 - 52 * y, 4), pl.ds(12 + 60 * y, 4)
    three_src, three_dst = pl.ds(69 - 53 * y, 3), pl.ds(13 + 59 * y, 3)

    def remote(src, dst, send, recv, device):
        return pltpu.make_async_remote_copy(src, dst, send, recv, device_id=device, device_id_type=MESH)

    def part(planes, rows):
        return e.at[all_tiles, planes, rows, :]

    side_copies = [
        remote(part(pl.ds(4, 8), four_src), part(pl.ds(4, 8), four_dst), side_send.at[0], side_recv.at[0], side),
        remote(part(pl.ds(9, 3), three_src), part(pl.ds(1, 3), three_dst), side_send.at[1], side_recv.at[1], side_up),
        remote(part(pl.ds(4, 3), three_src), part(pl.ds(12, 3), three_dst), side_send.at[2], side_recv.at[2], side_down),
    ]
    up_copies, down_copies = [], []
    for d in range(1, DEEP + 1):
        to_up, to_down = DEEP - d, DEEP + CZ - 1 + d
        up_copies.append(
            remote(part(to_up + CZ, mine_rows), part(to_up, mine_rows), lo_send.at[d - 1], lo_recv.at[d - 1], up)
        )
        down_copies.append(
            remote(part(to_down - CZ, mine_rows), part(to_down, mine_rows), hi_send.at[d - 1], hi_recv.at[d - 1], down)
        )

    one_src, one_dst = pl.ds(71 - 55 * y, 1), pl.ds(15 + 57 * y, 1)

    def ud_part(planes, rows):
        return ud.at[pl.ds(0, 2), all_tiles, planes, rows, :]

    inner = pl.ds(1, CZ)
    ud_copies = [
        remote(ud_part(CZ, mine_rows), ud_part(0, mine_rows), ud_send.at[0], ud_recv.at[0], up),
        remote(ud_part(1, mine_rows), ud_part(CZ + 1, mine_rows), ud_send.at[1], ud_recv.at[1], down),
        remote(ud_part(inner, one_src), ud_part(inner, one_dst), ud_send.at[2], ud_recv.at[2], side),
        remote(ud_part(CZ, one_src), ud_part(0, one_dst), ud_send.at[3], ud_recv.at[3], side_up),
        remote(ud_part(1, one_src), ud_part(CZ + 1, one_dst), ud_send.at[4], ud_recv.at[4], side_down),
    ]

    def sweep_lines(plane, rows, size, keep=None):
        fields = ([], [], [])
        for j in range(TILES):
            density = ud[1, j, plane, rows, :]
            field = ud[0, j, plane, rows, :]
            value = stiff_floor + (1.0 - stiff_floor) * (density * density * density)
            if keep is not None:
                value = value * keep
                field = field * keep
            fields[0].append(value)
            fields[1].append(field)
            fields[2].append(value * field)
        for slot in range(3):
            for j, tile in enumerate(smooth_lanes(fields[slot])):
                smooth[slot, j, plane, rows, :] = tile
        return fields[0]

    def sweep_own(plane, _):
        for k in range(CY // 16):
            rows = pl.ds(pl.multiple_of(own + 16 * k, 8), 16)
            for j, tile in enumerate(sweep_lines(plane, rows, 16)):
                stiff[j, plane, rows, :] = tile
        return 0

    def volume_plane(plane, total):
        for j in range(TILES):
            here = lab_out[plane, :, 128 * j : 128 * j + 128] == 0
            value = jnp.where(here, ud[1, j, plane + 1, mine_rows, :], 0.0)
            total = total + jnp.sum(value.reshape(CY // 8, 8, 128), axis=0)
        return total

    pl.semaphore_wait(barrier, len(greeted))
    for copy in (up_copies[0], down_copies[0]):
        copy.start()
    for copy in side_copies:
        copy.start()
    for copy in loads[3:]:
        copy.wait()
    volume = lax.fori_loop(0, CZ, volume_plane, jnp.zeros((8, 128), F32))
    for copy in (up_copies[0], down_copies[0]):
        copy.wait_send()
    for copy in (up_copies[1], down_copies[1]):
        copy.start()
    lax.fori_loop(1, 3, sweep_own, 0)
    for copy in (up_copies[1], down_copies[1]):
        copy.wait_send()
    for copy in (up_copies[2], down_copies[2]):
        copy.start()
    lax.fori_loop(3, 5, sweep_own, 0)
    for copy in (up_copies[2], down_copies[2]):
        copy.wait_send()
    for copy in (up_copies[3], down_copies[3]):
        copy.start()
    lax.fori_loop(5, 7, sweep_own, 0)
    for copy in ud_copies:
        copy.start()
    lax.fori_loop(7, CZ + 1, sweep_own, 0)

    def across(ref, j, plane, start, rows):
        over = ref[j, plane - 1, pl.ds(start, rows), :] + ref[j, plane + 1, pl.ds(start, rows), :]
        return over + (ref[j, plane, pl.ds(start - 1, rows), :] + ref[j, plane, pl.ds(start + 1, rows), :])

    def factor(row, j, rows):
        return jnp.broadcast_to(factors[row : row + 1, 128 * j : 128 * j + 128], (rows, 128))

    body = pl.ds(8, 72)

    def put(ref, j, plane, value, keep):
        ref[j, plane, body, :] = value if keep is None else value * keep

    def level3(plane, keep=None):
        for j in range(TILES):
            value = factor(0, j, 72) * e[j, plane, body, :] - (2.0 * NEAR * GAMMA[4]) * across(e, j, plane, 8, 72)
            put(b3, j, plane, value, keep)

    def level2(plane, keep=None):
        for j in range(TILES):
            value = (GAMMA[2] - GAMMA[4]) * e[j, plane, body, :] + factor(1, j, 72) * b3[j, plane, body, :]
            put(b2, j, plane, value - (2.0 * NEAR) * across(b3, j, plane, 8, 72), keep)

    def level1(plane, keep=None):
        for j in range(TILES):
            value = GAMMA[1] * e[j, plane, body, :] + factor(1, j, 72) * b2[j, plane, body, :]
            value = value - b3[j, plane, body, :]
            put(b1, j, plane, value - (2.0 * NEAR) * across(b2, j, plane, 8, 72), keep)

    def level0(plane, slot):
        for j in range(TILES):
            value = GAMMA[0] * e[j, plane, mine_rows, :] + factor(2, j, CY) * b1[j, plane, mine_rows, :]
            value = value - b2[j, plane, mine_rows, :]
            flat[slot, :, 128 * j : 128 * j + 128] = value - NEAR * across(b1, j, plane, own, CY)

    def repeat(level, first, last):
        def step(plane, _):
            level(plane)
            return 0

        lax.fori_loop(first, last, step, 0)

    side_copies[0].wait_recv()
    repeat(level3, 5, 11)
    repeat(level2, 6, 10)
    repeat(level1, 7, 9)
    side_copies[1].wait_recv()
    side_copies[2].wait_recv()

    low_keep = jnp.where(z == 0, 0.0, 1.0).astype(F32)
    high_keep = jnp.where(z == GZ - 1, 0.0, 1.0).astype(F32)

    def keep_of(plane):
        return low_keep if plane < DEEP else high_keep if plane >= DEEP + CZ else None

    def back(first, count, planes, total):
        value = transform(flat[first : first + count].reshape(count * CY, NX), basis)
        for k, plane in enumerate(planes):
            kept = jnp.where(lab_out[plane] == 0, value[CY * k : CY * k + CY], 0.0)
            filt_out[plane] = kept
            total = total + jnp.sum(jnp.abs(kept).reshape(CY // 8, 8, NX), axis=0)
        return total

    total = jnp.zeros((8, NX), F32)
    order = []
    for d in range(1, DEEP + 1):
        up_copies[d - 1].wait_recv()
        down_copies[d - 1].wait_recv()

        @pl.when(z == 0)
        def _():
            e[:, DEEP - d] = jnp.zeros((TILES, ROWS, 128), F32)

        @pl.when(z == GZ - 1)
        def _():
            e[:, DEEP + CZ - 1 + d] = jnp.zeros((TILES, ROWS, 128), F32)

        for level, low in ((level3, 5 - d), (level2, 6 - d), (level1, 7 - d)):
            for plane in (low, FZ - 1 - low):
                level(plane, keep_of(plane))
        for low in (8 - d, FZ - 1 - (8 - d)):
            level0(low, len(order))
            order.append(low - DEEP)
        if d == DEEP - 1:
            total = back(0, 6, order, total)
    total = back(6, 2, order[6:], total)

    def fold(value):
        return jnp.sum(value, axis=0, keepdims=True)

    row = lax.broadcasted_iota(jnp.int32, (8, 128), 0)
    size = total[:, :128] + total[:, 128:256] + total[:, 256:384] + total[:, 384:]
    mine[0] = jnp.where(row < 4, fold(size), fold(volume))

    def spread(phase):
        for d in range(GROUP - 1):
            remote(mine.at[phase], got.at[phase, d], ar_send.at[phase], ar_recv.at[phase], groups[phase][d]).start()

    def gather(phase):
        pltpu.make_async_copy(got.at[phase], got.at[phase], ar_recv.at[phase]).wait()
        return mine[phase] + jnp.sum(got[phase], axis=0)

    spread(0)

    for copy in ud_copies:
        copy.wait_recv()

    for plane, keep in ((0, low_keep), (CZ + 1, high_keep)):
        for k in range(3):
            sweep_lines(plane, pl.ds(8 + 24 * k, 24), 24, keep)

    def sweep_partner(plane, _):
        sweep_lines(plane, partner, 8)
        return 0

    lax.fori_loop(1, CZ + 1, sweep_partner, 0)

    def sweep_out(plane, _):
        for slot in range(3):
            for j in range(TILES):
                column[slot, j, body, :] = smooth[slot, j, plane + 1, body, :] + 0.5 * (
                    smooth[slot, j, plane, body, :] + smooth[slot, j, plane + 2, body, :]
                )
        for j in range(TILES):
            lanes = slice(128 * j, 128 * j + 128)

            def stack(slot):
                return column[slot, j, mine_rows, :] + 0.5 * (
                    column[slot, j, pl.ds(own - 1, CY), :] + column[slot, j, pl.ds(own + 1, CY), :]
                )

            value = stiff[j, plane + 1, mine_rows, :]
            field = ud[0, j, plane + 1, mine_rows, :]
            diagonal = 6.0 * value + stack(0)
            offsum = value * (stack(1) - 2.0 * field) + stack(2)
            applied = diagonal * field - offsum
            updated = field + relax_omega * (load_v[plane, :, lanes] - applied) / diagonal
            adj_out[plane, :, lanes] = jnp.where(lab_out[plane, :, lanes] == 2, 0.0, updated)
        return 0

    lax.fori_loop(0, CZ // 4, sweep_out, 0)

    mine[1] = gather(0)
    spread(1)

    lax.fori_loop(CZ // 4, CZ, sweep_out, 0)

    tot_out[...] = gather(1)
    for phase in range(2):
        pltpu.make_async_copy(got.at[phase], got.at[phase], ar_send.at[phase]).wait()
    for copy in side_copies + ud_copies + up_copies[3:] + down_copies[3:]:
        copy.wait_send()


def last_kernel(filt, adj_in, labels, tot, dir_out, adj_out, held, sem):
    whole = pltpu.make_async_copy(adj_in, adj_out, sem.at[CZ])
    whole.start()
    cells = float(GZ * CZ * GY * CY * NX)
    magnitude = jnp.sum(tot[0:1, :], axis=1, keepdims=True)
    volume = jnp.sum(tot[4:5, :], axis=1, keepdims=True)
    scale = 1.0 / (magnitude / cells + epsilon)
    offset = volume_penalty * (volume / cells - volume_target)
    scale = jnp.broadcast_to(scale, (CY, NX))
    offset = jnp.broadcast_to(offset, (CY, NX))
    copies = []
    for plane in range(CZ):
        held[plane] = jnp.where(labels[plane] == 0, filt[plane] * scale - offset, 0.0)
        copy = pltpu.make_async_copy(held.at[plane], dir_out.at[plane], sem.at[plane])
        copy.start()
        copies.append(copy)
    for copy in copies + [whole]:
        copy.wait()


def on_device(sensitivity, density, load, adjoint, labels):
    shape = (CZ, CY, NX)
    dma = pltpu.SemaphoreType.DMA
    vmem = pl.BlockSpec(memory_space=pltpu.VMEM)
    hbm = pl.BlockSpec(memory_space=pltpu.HBM)
    arrays = (sensitivity, density, load, adjoint, labels, jnp.asarray(BASIS), jnp.asarray(FACTORS))
    filtered, swept, held_labels, totals = pl.pallas_call(
        main_kernel,
        out_shape=(
            pltpu.VMEM(shape, F32),
            pltpu.VMEM(shape, F32),
            pltpu.VMEM(shape, jnp.int32),
            pltpu.VMEM((8, 128), F32),
        ),
        in_specs=[hbm] * 7,
        out_specs=(vmem,) * 4,
        scratch_shapes=[
            pltpu.VMEM(shape, F32),
            pltpu.VMEM((2, NX, NX), jnp.bfloat16),
            pltpu.VMEM((8, NX), F32),
            pltpu.VMEM((TILES, FZ, ROWS, 128), F32),
            pltpu.VMEM((TILES, FZ, ROWS, 128), F32),
            pltpu.VMEM((TILES, FZ, ROWS, 128), F32),
            pltpu.VMEM((TILES, FZ, ROWS, 128), F32),
            pltpu.VMEM(shape, F32),
            pltpu.VMEM((2, TILES, CZ + 2, ROWS, 128), F32),
            pltpu.VMEM((TILES, CZ + 2, ROWS, 128), F32),
            pltpu.VMEM((3, TILES, CZ + 2, ROWS, 128), F32),
            pltpu.VMEM((3, TILES, ROWS, 128), F32),
            pltpu.VMEM(shape, F32),
            pltpu.VMEM((2, 8, 128), F32),
            pltpu.VMEM((2, GROUP - 1, 8, 128), F32),
            dma((5 + 2 * TILES,)),
            dma((DEEP,)),
            dma((DEEP,)),
            dma((DEEP,)),
            dma((DEEP,)),
            dma((3,)),
            dma((3,)),
            dma((5,)),
            dma((5,)),
            dma((2,)),
            dma((2,)),
        ],
        compiler_params=pltpu.CompilerParams(
            collective_id=1, has_side_effects=True, vmem_limit_bytes=40 * 2**20
        ),
        name="filter_and_sweep",
    )(*[pltpu.with_memory_space_constraint(array, pltpu.HBM) for array in arrays])
    filtered, swept, held_labels, totals = (
        pltpu.with_memory_space_constraint(array, pltpu.VMEM) for array in (filtered, swept, held_labels, totals)
    )
    return pl.pallas_call(
        last_kernel,
        out_shape=(jax.ShapeDtypeStruct(shape, F32), jax.ShapeDtypeStruct(shape, F32)),
        in_specs=[vmem] * 4,
        out_specs=(hbm, hbm),
        scratch_shapes=[pltpu.VMEM(shape, F32), dma((CZ + 1,))],
        name="normalise_and_store",
    )(filtered, swept, held_labels, totals)


def solution(mesh):
    placed = (P("gz", "gy", None),) * 5
    return jax.shard_map(
        on_device,
        mesh=mesh,
        in_specs=placed,
        out_specs=(P("gz", "gy", None), P("gz", "gy", None)),
        check_vma=False,
    )
```

time: 51.7 us -> 34.7 us (0.67); the launches traced: 50.8 us -> 34.6 us
  local copies, waits for them, and re-layouts: 9.66 us -> 0 us
  Pallas kernels: 40.5 us -> 34 us
    unnamed x18 -> x0, local copies, waits for them, and re-layouts: 9.66 us -> none
    pallas_call x1, Pallas kernels: 37.2 us -> 32.6 us  [on_device(): pl.pallas_call(main_kernel, out_shape=(pltpu.VMEM(shape, F32), pltpu.VMEM...]
    pallas_call x1, Pallas kernels: 3.24 us -> 1.38 us  [on_device(): pl.pallas_call(last_kernel, out_shape=(jax.ShapeDtypeStruct(shape, F32),...]
where the time goes in v2:
time: 34.7 us; the launch traced here: 34.6 us
  Pallas kernels  34 us (98%)
  between operations  0.64 us (2%)
    pallas_call x1, Pallas kernels, on_device(): pl.pallas_call(main_kernel, out_shape=(pltpu.VMEM(shape, F32), pltpu.VMEM...  32.6 us
    pallas_call x1, Pallas kernels, on_device(): pl.pallas_call(last_kernel, out_shape=(jax.ShapeDtypeStruct(shape, F32),...  1.38 us

profile of v2, /device:TPU:1, one launch (start us, length us, event | category | flops | bytes accessed | tf_op | source)
XLA Modules:
  0.0 34.6 jit_solution(3601178954657687840)
XLA Ops:
  0.6 32.6 %filter_and_sweep.1 = (f32[8,64,512]{2,1,0:T(8,128)S(1)}, f32[8,64,512]{2,1,0:T(8,128)S(1)}, s32[8,64,512]{2,1,0:T(8,128)S(1)}, f32[8,128]{1,0:T(8,128)S(1)}) custom-call(f32[8,64,512]{2,1,0:T(8,128)} %sens.1, f32[8,64,512]{2,1,0:T(8,128)} %dens.1, f32[8,64,512]{2,1,0:T(8,128)} %load.1, f32[8,64,512]{2,1,0:T(8,128)} %adj.1, s32[8,64,512]{2,1,0:T(8,128)} %labels.1, ...), custom_call_target="tpu_custom_call" | custom-call | tf_op jit(solution)/shard_map/filter_and_sweep/pallas_call | solution.py:453
  33.2 1.4 %normalise_and_store.1 = (f32[8,64,512]{2,1,0:T(8,128)}, f32[8,64,512]{2,1,0:T(8,128)}) custom-call(f32[8,64,512]{2,1,0:T(8,128)S(1)} %get-tuple-element.6.filt, f32[8,64,512]{2,1,0:T(8,128)S(1)} %get-tuple-element.7.adj_in, s32[8,64,512]{2,1,0:T(8,128)S(1)} %get-tuple-element.8.labels, f32[8,128]{1,0:T(8,128)S(1)} %get-tuple-element.9.tot), custom_call_target="tpu_custom_call" | custom-call | tf_op jit(solution)/shard_map/normalise_and_store/pallas_call | solution.py:499

commit v3 on v2

--- a/solution.py
+++ b/solution.py
@@ -31,6 +31,8 @@
 ROWS = CY + 24
 DEEP = ITERS
 FZ = CZ + 2 * DEEP
+PIECES = (2, 1, 1)
+FIRSTS = {1: 0, 3: 1, 4: 2}
 
 
 def filter_coefficients():
@@ -143,7 +145,7 @@
                     in_sem.at[5 + 2 * j + slot],
                 )
             )
-    for copy in loads:
+    for copy in loads[:3]:
         copy.start()
 
     e[:, :, partner, :] = jnp.zeros((TILES, FZ, 8, 128), F32)
@@ -153,6 +155,8 @@
     greeted = [up, down, side, side_up, side_down] + groups[0] + groups[1]
     for device in greeted:
         pl.semaphore_signal(barrier, inc=1, device_id=device, device_id_type=MESH)
+    for copy in loads[3:]:
+        copy.start()
 
     def clear(j, _):
         for ref in (e, b3, b2, b1):
@@ -190,14 +194,23 @@
         remote(part(pl.ds(4, 3), three_src), part(pl.ds(12, 3), three_dst), side_send.at[2], side_recv.at[2], side_down),
     ]
     up_copies, down_copies = [], []
-    for d in range(1, DEEP + 1):
-        to_up, to_down = DEEP - d, DEEP + CZ - 1 + d
-        up_copies.append(
-            remote(part(to_up + CZ, mine_rows), part(to_up, mine_rows), lo_send.at[d - 1], lo_recv.at[d - 1], up)
+    near = 0
+    for at, count in enumerate(PIECES):
+        low, high = pl.ds(DEEP - near - count, count), pl.ds(DEEP + CZ + near, count)
+        low_src, high_src = pl.ds(DEEP + CZ - near - count, count), pl.ds(DEEP + near, count)
+        up_copies.append(remote(part(low_src, mine_rows), part(low, mine_rows), lo_send.at[at], lo_recv.at[at], up))
+        down_copies.append(
+            remote(part(high_src, mine_rows), part(high, mine_rows), hi_send.at[at], hi_recv.at[at], down)
         )
-        down_copies.append(
-            remote(part(to_down - CZ, mine_rows), part(to_down, mine_rows), hi_send.at[d - 1], hi_recv.at[d - 1], down)
-        )
+        near += count
+
+    def start(piece):
+        up_copies[piece].start()
+        down_copies[piece].start()
+
+    def sent(piece):
+        up_copies[piece].wait_send()
+        down_copies[piece].wait_send()
 
     one_src, one_dst = pl.ds(71 - 55 * y, 1), pl.ds(15 + 57 * y, 1)
 
@@ -245,31 +258,18 @@
         return total
 
     pl.semaphore_wait(barrier, len(greeted))
-    for copy in (up_copies[0], down_copies[0]):
-        copy.start()
+    start(0)
     for copy in side_copies:
         copy.start()
     for copy in loads[3:]:
         copy.wait()
     volume = lax.fori_loop(0, CZ, volume_plane, jnp.zeros((8, 128), F32))
-    for copy in (up_copies[0], down_copies[0]):
-        copy.wait_send()
-    for copy in (up_copies[1], down_copies[1]):
-        copy.start()
-    lax.fori_loop(1, 3, sweep_own, 0)
-    for copy in (up_copies[1], down_copies[1]):
-        copy.wait_send()
-    for copy in (up_copies[2], down_copies[2]):
-        copy.start()
-    lax.fori_loop(3, 5, sweep_own, 0)
-    for copy in (up_copies[2], down_copies[2]):
-        copy.wait_send()
-    for copy in (up_copies[3], down_copies[3]):
-        copy.start()
-    lax.fori_loop(5, 7, sweep_own, 0)
-    for copy in ud_copies:
-        copy.start()
-    lax.fori_loop(7, CZ + 1, sweep_own, 0)
+    lax.fori_loop(1, 4, sweep_own, 0)
+    sent(0)
+    start(1)
+    lax.fori_loop(4, 6, sweep_own, 0)
+    sent(1)
+    start(2)
 
     def across(ref, j, plane, start, rows):
         over = ref[j, plane - 1, pl.ds(start, rows), :] + ref[j, plane + 1, pl.ds(start, rows), :]
@@ -319,6 +319,9 @@
     side_copies[1].wait_recv()
     side_copies[2].wait_recv()
 
+    sent(2)
+    for copy in ud_copies:
+        copy.start()
     low_keep = jnp.where(z == 0, 0.0, 1.0).astype(F32)
     high_keep = jnp.where(z == GZ - 1, 0.0, 1.0).astype(F32)
 
@@ -336,8 +339,9 @@
     total = jnp.zeros((8, NX), F32)
     order = []
     for d in range(1, DEEP + 1):
-        up_copies[d - 1].wait_recv()
-        down_copies[d - 1].wait_recv()
+        if d in FIRSTS:
+            up_copies[FIRSTS[d]].wait_recv()
+            down_copies[FIRSTS[d]].wait_recv()
 
         @pl.when(z == 0)
         def _():
@@ -374,19 +378,7 @@
 
     spread(0)
 
-    for copy in ud_copies:
-        copy.wait_recv()
-
-    for plane, keep in ((0, low_keep), (CZ + 1, high_keep)):
-        for k in range(3):
-            sweep_lines(plane, pl.ds(8 + 24 * k, 24), 24, keep)
-
-    def sweep_partner(plane, _):
-        sweep_lines(plane, partner, 8)
-        return 0
-
-    lax.fori_loop(1, CZ + 1, sweep_partner, 0)
-
+    lax.fori_loop(6, CZ + 1, sweep_own, 0)
     def sweep_out(plane, _):
         for slot in range(3):
             for j in range(TILES):
@@ -410,17 +402,28 @@
             adj_out[plane, :, lanes] = jnp.where(lab_out[plane, :, lanes] == 2, 0.0, updated)
         return 0
 
-    lax.fori_loop(0, CZ // 4, sweep_out, 0)
-
     mine[1] = gather(0)
     spread(1)
 
-    lax.fori_loop(CZ // 4, CZ, sweep_out, 0)
+    for copy in ud_copies:
+        copy.wait_recv()
+
+    for plane, keep in ((0, low_keep), (CZ + 1, high_keep)):
+        for k in range(3):
+            sweep_lines(plane, pl.ds(8 + 24 * k, 24), 24, keep)
+
+    def sweep_partner(plane, _):
+        sweep_lines(plane, partner, 8)
+        return 0
+
+    lax.fori_loop(1, CZ + 1, sweep_partner, 0)
+
+    lax.fori_loop(0, CZ, sweep_out, 0)
 
     tot_out[...] = gather(1)
     for phase in range(2):
         pltpu.make_async_copy(got.at[phase], got.at[phase], ar_send.at[phase]).wait()
-    for copy in side_copies + ud_copies + up_copies[3:] + down_copies[3:]:
+    for copy in side_copies + ud_copies:
         copy.wait_send()
 
 
@@ -477,10 +480,10 @@
             pltpu.VMEM((2, 8, 128), F32),
             pltpu.VMEM((2, GROUP - 1, 8, 128), F32),
             dma((5 + 2 * TILES,)),
-            dma((DEEP,)),
-            dma((DEEP,)),
-            dma((DEEP,)),
-            dma((DEEP,)),
+            dma((len(PIECES),)),
+            dma((len(PIECES),)),
+            dma((len(PIECES),)),
+            dma((len(PIECES),)),
             dma((3,)),
             dma((3,)),
             dma((5,)),

time: 34.7 us -> 33.9 us (0.977)
  Pallas kernels: 34 us -> 33.2 us
    pallas_call x1, Pallas kernels: 32.6 us -> 31.8 us  [on_device(): pl.pallas_call(main_kernel, out_shape=(pltpu.VMEM(shape, F32), pltpu.VMEM...]
where the time goes in v3:
time: 33.9 us; the launch traced here: 33.8 us
  Pallas kernels  33.2 us (98%)
  between operations  0.64 us (2%)
    pallas_call x1, Pallas kernels, on_device(): pl.pallas_call(main_kernel, out_shape=(pltpu.VMEM(shape, F32), pltpu.VMEM...  31.8 us
    pallas_call x1, Pallas kernels, on_device(): pl.pallas_call(last_kernel, out_shape=(jax.ShapeDtypeStruct(shape, F32),...  1.38 us

profile of v3, /device:TPU:1, one launch (start us, length us, event | category | flops | bytes accessed | tf_op | source)
XLA Modules:
  0.0 33.8 jit_solution(11956299192778212406)
XLA Ops:
  0.6 31.8 %filter_and_sweep.1 = (f32[8,64,512]{2,1,0:T(8,128)S(1)}, f32[8,64,512]{2,1,0:T(8,128)S(1)}, s32[8,64,512]{2,1,0:T(8,128)S(1)}, f32[8,128]{1,0:T(8,128)S(1)}) custom-call(f32[8,64,512]{2,1,0:T(8,128)} %sens.1, f32[8,64,512]{2,1,0:T(8,128)} %dens.1, f32[8,64,512]{2,1,0:T(8,128)} %load.1, f32[8,64,512]{2,1,0:T(8,128)} %adj.1, s32[8,64,512]{2,1,0:T(8,128)} %labels.1, ...), custom_call_target="tpu_custom_call" | custom-call | tf_op jit(solution)/shard_map/filter_and_sweep/pallas_call | solution.py:456
  32.4 1.4 %normalise_and_store.1 = (f32[8,64,512]{2,1,0:T(8,128)}, f32[8,64,512]{2,1,0:T(8,128)}) custom-call(f32[8,64,512]{2,1,0:T(8,128)S(1)} %get-tuple-element.6.filt, f32[8,64,512]{2,1,0:T(8,128)S(1)} %get-tuple-element.7.adj_in, s32[8,64,512]{2,1,0:T(8,128)S(1)} %get-tuple-element.8.labels, f32[8,128]{1,0:T(8,128)S(1)} %get-tuple-element.9.tot), custom_call_target="tpu_custom_call" | custom-call | tf_op jit(solution)/shard_map/normalise_and_store/pallas_call | solution.py:502

commit v4 on v3

--- a/solution.py
+++ b/solution.py
@@ -66,6 +66,20 @@
 TILES = NX // 128
 
 
+def hops(*offsets):
+    return sum(min(offset, size - offset) for offset, size in offsets)
+
+
+LINE = sorted(
+    [(dz, dc) for dz in range(8) for dc in range(2) if dz or dc],
+    key=lambda at: (-hops((at[0], 8)), at),
+)
+PLANE = sorted(
+    [(dy, dx) for dy in range(4) for dx in range(4) if dy or dx],
+    key=lambda at: (-hops((at[0], 4), (at[1], 4)), at),
+)
+
+
 def sine_basis():
     index = np.arange(1, NX + 1, dtype=np.float64)
     basis = np.sqrt(2.0 / (NX + 1)) * np.sin(np.pi * np.outer(index, index) / (NX + 1))
@@ -107,7 +121,7 @@
     sens, dens, load, adj, labels, basis_in, factors_in,
     filt_out, adj_out, lab_out, tot_out,
     raw, basis, factors, e, b3, b2, b1, flat, ud, stiff, smooth, column, load_v, mine, got,
-    in_sem, lo_send, lo_recv, hi_send, hi_recv, side_send, side_recv, ud_send, ud_recv, ar_send, ar_recv,
+    in_sem, lo_send, lo_recv, hi_send, hi_recv, side_send, side_recv, ud_send, ud_recv, ar_send, ar_recv, met,
 ):
     z = lax.axis_index("gz")
     y = lax.axis_index("gy")
@@ -118,12 +132,28 @@
     side_down = (down[0], 1 - y)
     block = z // GROUP
     rank = lax.rem(z, GROUP)
-    plane_rank = block * GY + y
+    chip, core = rank // 2, lax.rem(rank, 2)
+    across_y, across_x = block // 2, 2 * y + lax.rem(block, 2)
     groups = ([], [])
-    for d in range(1, GROUP):
-        groups[0].append((block * GROUP + lax.rem(rank + d, GROUP), y))
-        other = lax.rem(plane_rank + d, GROUP)
-        groups[1].append(((other // GY) * GROUP + rank, lax.rem(other, GY)))
+    for dz, dc in LINE:
+        groups[0].append((block * GROUP + 2 * lax.rem(chip + dz, 8) + lax.rem(core + dc, 2), y))
+    for dy, dx in PLANE:
+        other_y, other_x = lax.rem(across_y + dy, 4), lax.rem(across_x + dx, 4)
+        groups[1].append(((2 * other_y + lax.rem(other_x, 2)) * GROUP + rank, other_x // 2))
+
+    near = [(block * GROUP + lax.rem(rank + d, GROUP), y) for d in (1, 2, 14, 15)]
+    at_y, at_x = block // 2, 2 * y + lax.rem(block, 2)
+    for dy, dx in ((0, 1), (0, 3), (1, 0), (3, 0)):
+        to_y, to_x = lax.rem(at_y + dy, 4), lax.rem(at_x + dx, 4)
+        near.append(((2 * to_y + lax.rem(to_x, 2)) * GROUP + rank, to_x // 2))
+    told = near + [side]
+
+    def tell(turn):
+        for device in told:
+            pl.semaphore_signal(met.at[turn], inc=1, device_id=device, device_id_type=MESH)
+
+    def heard(turn):
+        pl.semaphore_wait(met.at[turn], len(told))
 
     own = pl.multiple_of(8 + 8 * y, 8)
     mine_rows = pl.ds(own, CY)
@@ -152,7 +182,7 @@
     ud[:, :, :, partner, :] = jnp.zeros((2, TILES, CZ + 2, 8, 128), F32)
 
     barrier = pltpu.get_barrier_semaphore()
-    greeted = [up, down, side, side_up, side_down] + groups[0] + groups[1]
+    greeted = [up, down, side, side_up, side_down] + near
     for device in greeted:
         pl.semaphore_signal(barrier, inc=1, device_id=device, device_id_type=MESH)
     for copy in loads[3:]:
@@ -168,8 +198,6 @@
             column[slot, j, 0:8, :] = jnp.zeros((8, 128), F32)
             column[slot, j, 80:88, :] = jnp.zeros((8, 128), F32)
         return 0
-
-    lax.fori_loop(0, TILES, clear, 0)
 
     loads[0].wait()
     loads[1].wait()
@@ -261,6 +289,8 @@
     start(0)
     for copy in side_copies:
         copy.start()
+    tell(0)
+    lax.fori_loop(0, TILES, clear, 0)
     for copy in loads[3:]:
         copy.wait()
     volume = lax.fori_loop(0, CZ, volume_plane, jnp.zeros((8, 128), F32))
@@ -270,6 +300,8 @@
     lax.fori_loop(4, 6, sweep_own, 0)
     sent(1)
     start(2)
+    heard(0)
+    tell(1)
 
     def across(ref, j, plane, start, rows):
         over = ref[j, plane - 1, pl.ds(start, rows), :] + ref[j, plane + 1, pl.ds(start, rows), :]
@@ -318,6 +350,8 @@
     repeat(level1, 7, 9)
     side_copies[1].wait_recv()
     side_copies[2].wait_recv()
+    heard(1)
+    tell(2)
 
     sent(2)
     for copy in ud_copies:
@@ -376,6 +410,7 @@
         pltpu.make_async_copy(got.at[phase], got.at[phase], ar_recv.at[phase]).wait()
         return mine[phase] + jnp.sum(got[phase], axis=0)
 
+    heard(2)
     spread(0)
 
     lax.fori_loop(6, CZ + 1, sweep_own, 0)
@@ -490,6 +525,7 @@
             dma((5,)),
             dma((2,)),
             dma((2,)),
+            pltpu.SemaphoreType.REGULAR((3,)),
         ],
         compiler_params=pltpu.CompilerParams(
             collective_id=1, has_side_effects=True, vmem_limit_bytes=40 * 2**20

time: 33.9 us -> 33.3 us (0.982)
  Pallas kernels: 33.2 us -> 32.6 us
    pallas_call x1, Pallas kernels: 31.8 us -> 31.2 us  [on_device(): pl.pallas_call(main_kernel, out_shape=(pltpu.VMEM(shape, F32), pltpu.VMEM...]
where the time goes in v4:
time: 33.3 us; the launch traced here: 33.2 us
  Pallas kernels  32.6 us (98%)
  between operations  0.64 us (2%)
    pallas_call x1, Pallas kernels, on_device(): pl.pallas_call(main_kernel, out_shape=(pltpu.VMEM(shape, F32), pltpu.VMEM...  31.2 us
    pallas_call x1, Pallas kernels, on_device(): pl.pallas_call(last_kernel, out_shape=(jax.ShapeDtypeStruct(shape, F32),...  1.38 us

profile of v4, /device:TPU:1, one launch (start us, length us, event | category | flops | bytes accessed | tf_op | source)
XLA Modules:
  0.0 33.2 jit_solution(13546767057284738048)
XLA Ops:
  0.6 31.2 %filter_and_sweep.1 = (f32[8,64,512]{2,1,0:T(8,128)S(1)}, f32[8,64,512]{2,1,0:T(8,128)S(1)}, s32[8,64,512]{2,1,0:T(8,128)S(1)}, f32[8,128]{1,0:T(8,128)S(1)}) custom-call(f32[8,64,512]{2,1,0:T(8,128)} %sens.1, f32[8,64,512]{2,1,0:T(8,128)} %dens.1, f32[8,64,512]{2,1,0:T(8,128)} %load.1, f32[8,64,512]{2,1,0:T(8,128)} %adj.1, s32[8,64,512]{2,1,0:T(8,128)} %labels.1, ...), custom_call_target="tpu_custom_call" | custom-call | tf_op jit(solution)/shard_map/filter_and_sweep/pallas_call | solution.py:491
  31.9 1.4 %normalise_and_store.1 = (f32[8,64,512]{2,1,0:T(8,128)}, f32[8,64,512]{2,1,0:T(8,128)}) custom-call(f32[8,64,512]{2,1,0:T(8,128)S(1)} %get-tuple-element.6.filt, f32[8,64,512]{2,1,0:T(8,128)S(1)} %get-tuple-element.7.adj_in, s32[8,64,512]{2,1,0:T(8,128)S(1)} %get-tuple-element.8.labels, f32[8,128]{1,0:T(8,128)S(1)} %get-tuple-element.9.tot), custom_call_target="tpu_custom_call" | custom-call | tf_op jit(solution)/shard_map/normalise_and_store/pallas_call | solution.py:538

commit v5 on v4

--- a/solution.py
+++ b/solution.py
@@ -31,8 +31,8 @@
 ROWS = CY + 24
 DEEP = ITERS
 FZ = CZ + 2 * DEEP
-PIECES = (2, 1, 1)
-FIRSTS = {1: 0, 3: 1, 4: 2}
+PIECES = (2, 2)
+FIRSTS = {1: 0, 3: 1}
 
 
 def filter_coefficients():
@@ -298,8 +298,6 @@
     sent(0)
     start(1)
     lax.fori_loop(4, 6, sweep_own, 0)
-    sent(1)
-    start(2)
     heard(0)
     tell(1)
 
@@ -353,7 +351,7 @@
     heard(1)
     tell(2)
 
-    sent(2)
+    sent(1)
     for copy in ud_copies:
         copy.start()
     low_keep = jnp.where(z == 0, 0.0, 1.0).astype(F32)

time: 33.3 us -> 33 us (level)
  Pallas kernels: 32.6 us -> 32.2 us
    pallas_call x1, Pallas kernels: 31.2 us -> 30.9 us  [on_device(): pl.pallas_call(main_kernel, out_shape=(pltpu.VMEM(shape, F32), pltpu.VMEM...]
where the time goes in v5:
time: 33 us; the launch traced here: 32.9 us
  Pallas kernels  32.2 us (98%)
  between operations  0.64 us (2%)
    pallas_call x1, Pallas kernels, on_device(): pl.pallas_call(main_kernel, out_shape=(pltpu.VMEM(shape, F32), pltpu.VMEM...  30.9 us
    pallas_call x1, Pallas kernels, on_device(): pl.pallas_call(last_kernel, out_shape=(jax.ShapeDtypeStruct(shape, F32),...  1.38 us

profile of v5, /device:TPU:1, one launch (start us, length us, event | category | flops | bytes accessed | tf_op | source)
XLA Modules:
  0.0 32.9 jit_solution(12337212072025918550)
XLA Ops:
  0.6 30.9 %filter_and_sweep.1 = (f32[8,64,512]{2,1,0:T(8,128)S(1)}, f32[8,64,512]{2,1,0:T(8,128)S(1)}, s32[8,64,512]{2,1,0:T(8,128)S(1)}, f32[8,128]{1,0:T(8,128)S(1)}) custom-call(f32[8,64,512]{2,1,0:T(8,128)} %sens.1, f32[8,64,512]{2,1,0:T(8,128)} %dens.1, f32[8,64,512]{2,1,0:T(8,128)} %load.1, f32[8,64,512]{2,1,0:T(8,128)} %adj.1, s32[8,64,512]{2,1,0:T(8,128)} %labels.1, ...), custom_call_target="tpu_custom_call" | custom-call | tf_op jit(solution)/shard_map/filter_and_sweep/pallas_call | solution.py:489
  31.5 1.4 %normalise_and_store.1 = (f32[8,64,512]{2,1,0:T(8,128)}, f32[8,64,512]{2,1,0:T(8,128)}) custom-call(f32[8,64,512]{2,1,0:T(8,128)S(1)} %get-tuple-element.6.filt, f32[8,64,512]{2,1,0:T(8,128)S(1)} %get-tuple-element.7.adj_in, s32[8,64,512]{2,1,0:T(8,128)S(1)} %get-tuple-element.8.labels, f32[8,128]{1,0:T(8,128)S(1)} %get-tuple-element.9.tot), custom_call_target="tpu_custom_call" | custom-call | tf_op jit(solution)/shard_map/normalise_and_store/pallas_call | solution.py:536
